TPU v7x, 32 devices: a whole 2x2x4 slice. The times are simulated.
32 devices in a mesh: rep: 2 (over x), node: 2 (over core), ep: 8 (over z, y).
Axes of the slice: x: 2, y: 2, z: 4, core: 2. Of those that a mesh axis runs over, the one named last changes fastest.
Arguments:
- activations: bfloat16 [3072, 7168], P(('rep', 'node', 'ep')), parts along dimension 0, may hold values from -6 to 6
- expert_ids: int32 [3072, 8], P(('rep', 'node', 'ep')), parts along dimension 0, may hold values from 0 to 255, all different within a row; in each aligned block of 96 rows (0 to 95, 96 to 191, ...) at most 8 rows name the same one
- route_scores: float32 [3072, 8], P(('rep', 'node', 'ep')), parts along dimension 0, may hold values from 0.05 to 1
- capacity: int32 [256], replicated, may hold values from 6 to 8
- w_gate: bfloat16 [7168, 4096], P(None, ('node', 'ep')), may hold values from -0.0625 to 0.0625
- w_up: bfloat16 [7168, 4096], P(None, ('node', 'ep')), may hold values from -0.0625 to 0.0625
- w_down: bfloat16 [4096, 7168], P(('node', 'ep')), may hold values from -0.125 to 0.125
Outputs:
- mixed_out: bfloat16 [3072, 7168], P(('rep', 'node', 'ep')), parts along dimension 0
There are 2 independent parts, one for each index of `rep`. A program takes and returns all parts, laid end to end along the dimension named above; an argument that names none is the same for every part. Nothing has to cross between parts.
Inputs may be any that keep to these rules, and one draw needn't show every extreme that they name: `expert_ids`: each row names 8 different experts. In each aligned block of 96 rows (the rows of one device) no expert is named by more than 8 rows, and in some block one expert is named by exactly 8 rows.
All inputs are finite; a program needn't handle non-finite values.
Results may differ from a plain program's by a relative error of at most 0.007.
Values may be sent and summed in bfloat16 or wider, within the bound.
A program may use at most 128 MiB of HBM per device.

v0:
```python
import jax
import jax.numpy as jnp
from jax import lax
from jax.sharding import PartitionSpec as P

TOPK = 8
SHARDS = 8
SEND_CAP = 8


def shards(activations, expert_ids, route_scores, capacity, w_gate, w_up, w_down):
    n_node = lax.axis_size("node")
    n_ep = lax.axis_size("ep")
    window = n_node * (n_ep // SHARDS)
    tok_rows = activations.shape[0]
    model_width = activations.shape[1]
    send_cap = SEND_CAP
    route_weight = (2.5 * route_scores / jnp.sum(route_scores, axis=1, keepdims=True)).astype(
        jnp.bfloat16
    )
    flat_ids = expert_ids.reshape(-1)
    expert_iota = jnp.arange(window, dtype=jnp.int32)
    onehot = (flat_ids[:, None] == expert_iota[None, :]).astype(jnp.int32)
    running = jnp.cumsum(onehot, axis=0)
    ranking = jnp.sum(onehot * running, axis=1) - 1
    limits = jnp.sum(onehot * capacity[:window][None, :], axis=1)
    is_live = (flat_ids < window) & (ranking < limits)
    slot_index = jnp.where(is_live, ranking * window + flat_ids, -1).reshape(tok_rows, TOPK)
    positions = jnp.arange(send_cap * window, dtype=jnp.int32)
    matches = slot_index[:, :, None] == positions[None, None, :]
    select = jnp.any(matches, axis=1).astype(jnp.bfloat16)
    combine_w = jnp.sum(
        jnp.where(matches, route_weight[:, :, None].astype(jnp.float32), 0.0), axis=1
    ).astype(jnp.bfloat16)
    expert_rows = lax.dot_general(
        select, activations, (((0,), (0,)), ((), ())), preferred_element_type=jnp.float32
    ).astype(jnp.bfloat16)
    copies = jnp.broadcast_to(
        expert_rows.reshape(send_cap, window, 1, model_width),
        (send_cap, window, SHARDS, model_width),
    )
    copies = copies.reshape(send_cap, window * SHARDS * model_width)
    received = lax.all_to_all(copies, ("node", "ep"), split_axis=1, concat_axis=0, tiled=True)
    gate_act = jnp.dot(received, w_gate, preferred_element_type=jnp.float32)
    up_act = jnp.dot(received, w_up, preferred_element_type=jnp.float32)
    inner_act = (jax.nn.silu(gate_act) * up_act).astype(jnp.bfloat16)
    partial_value = jnp.dot(inner_act, w_down, preferred_element_type=jnp.float32).astype(
        jnp.bfloat16
    )
    returned = lax.all_to_all(
        partial_value, ("node", "ep"), split_axis=0, concat_axis=1, tiled=True
    )
    summed = jnp.sum(
        returned.reshape(send_cap, window, SHARDS, model_width).astype(jnp.float32), axis=2
    )
    expert_out = summed.astype(jnp.bfloat16).reshape(send_cap * window, model_width)
    mixed_out = jnp.dot(combine_w, expert_out, preferred_element_type=jnp.float32)
    return mixed_out.astype(jnp.bfloat16)


def solution(mesh):
    placed = (
        P(("rep", "node", "ep"), None),
        P(("rep", "node", "ep"), None),
        P(("rep", "node", "ep"), None),
        P(),
        P(None, ("node", "ep")),
        P(None, ("node", "ep")),
        P(("node", "ep"), None),
    )
    return jax.shard_map(
        shards,
        mesh=mesh,
        in_specs=placed,
        out_specs=P(("rep", "node", "ep"), None),
        check_vma=False,
    )
```

profile of v0, /device:TPU:0, one launch (start us, length us, event | category | flops | bytes accessed | tf_op | source)
XLA Modules:
  0.0 111.7 jit_solution(11825912123103637743)
XLA Ops:
  0.0 0.0 copy-start
  0.0 0.9 copy.40
  0.9 0.1 eq.42
  1.0 0.1 eq.38
  1.1 0.7 slice.11
  1.8 0.6 reduce-window.6
  2.3 0.2 slice_reduce_fusion
  2.5 0.2 reduce-window.9
  2.7 0.1 add_bitcast_fusion
  2.8 0.1 select_reduce_fusion.1
  2.9 0.1 lt.15
  3.0 0.1 copy.42
  3.1 0.1 mul.36
  3.2 0.1 copy.43
  3.3 0.7 add_select_fusion
  4.0 0.0 copy-done
  4.0 0.3 convolution_convert_fusion.2
  4.3 0.1 broadcast_in_dim.28
  4.4 0.2 broadcast_in_dim.29
  4.6 0.0 copy-start.1
  4.6 51.5 %all_to_all.35 = bf16[8,16,7168]{2,0,1:T(8,128)(2,1)S(1)} all-to-all(bf16[8,16,7168]{2,0,1:T(8,128)(2,1)S(1)} %bitcast.42), channel_id=1, replica_groups=mesh['rep'=2,'node'=2,'ep'=8] {'node','ep'}, dimensions={1} | all-to-all | bytes 3670016 | tf_op jit(solution)/shard_map/all_to_all | solution.py:43
  56.2 0.0 copy-done.1
  56.2 0.7 fusion.3
  56.8 6.5 %fusion = bf16[16,8,7168]{2,1,0:T(8,128)(2,1)} fusion(bf16[256,7168]{1,0:T(8,128)(2,1)} %param.13, bf16[7168,256]{1,0:T(8,128)(2,1)} %param.12, bf16[8,16,7168]{2,0,1:T(8,128)(2,1)S(1)} %all_to_all.35, f32[128,256]{1,0:T(8,128)S(1)} %fusion.3), kind=kOutput, calls=%fused_computation.2 | convolution fusion | flops 940638208 | bytes 11141120 | tf_op jit(solution)/shard_map/dot_general | solution.py:47
  63.4 0.0 copy-start.2
  63.4 3.8 %all-to-all-start.1 = ((bf16[16,8,7168]{2,1,0:T(8,128)(2,1)}), bf16[16,8,7168]{2,1,0:T(8,128)(2,1)S(1)}, u32[]{:S(2)}, u32[]{:S(2)}) async-start(bf16[16,8,7168]{2,1,0:T(8,128)(2,1)} %fusion), calls=%async_computation.1 | async-start | bytes 3670016 | tf_op jit(solution)/shard_map/all_to_all | solution.py:50
  67.2 0.0 copy-done.2
  67.3 42.1 %all-to-all-done.1 = bf16[16,8,7168]{2,1,0:T(8,128)(2,1)S(1)} async-done(((bf16[16,8,7168]{2,1,0:T(8,128)(2,1)}), bf16[16,8,7168]{2,1,0:T(8,128)(2,1)S(1)}, u32[]{:S(2)}, u32[]{:S(2)}) %all-to-all-start.1) | async-done | bytes 1835040 | tf_op jit(solution)/shard_map/all_to_all | solution.py:50
  109.5 0.2 bitcast_reduce_fusion
  109.7 0.2 copy.45
  109.9 0.1 reshape.59
  110.0 1.6 %convolution_convert_fusion.1 = bf16[96,7168]{1,0:T(8,128)(2,1)} fusion(bf16[16,7168]{1,0:T(8,128)(2,1)S(1)} %reshape.59, bf16[96,16]{0,1:T(8,128)(2,1)S(1)} %select_reduce_fusion), kind=kOutput, calls=%fused_computation.1 | convolution fusion | flops 22708224 | bytes 1608704 | tf_op jit(solution)/shard_map/dot_general | solution.py:57
  (8 shorter events, 0.1 us)
Async XLA Ops:
  0.0 4.0 %copy-start = (bf16[96,7168]{1,0:T(8,128)(2,1)S(1)}, bf16[96,7168]{1,0:T(8,128)(2,1)}, u32[]{:S(2)}) copy-start(bf16[96,7168]{1,0:T(8,128)(2,1)} %param.7) | copy-start | bytes 4128772
  4.6 51.5 %copy-start.1 = (bf16[7168,256]{1,0:T(8,128)(2,1)S(1)}, bf16[7168,256]{1,0:T(8,128)(2,1)}, u32[]{:S(2)}) copy-start(bf16[7168,256]{1,0:T(8,128)(2,1)} %param.11) | copy-start | bytes 11010052
  63.4 3.9 %copy-start.2 = (f32[96,8]{0,1:T(8,128)S(1)}, f32[96,8]{0,1:T(8,128)}, u32[]{:S(2)}) copy-start(f32[96,8]{0,1:T(8,128)} %param.9) | copy-start | bytes 9220
  63.4 46.1 %all-to-all-start.1 = ((bf16[16,8,7168]{2,1,0:T(8,128)(2,1)}), bf16[16,8,7168]{2,1,0:T(8,128)(2,1)S(1)}, u32[]{:S(2)}, u32[]{:S(2)}) async-start(bf16[16,8,7168]{2,1,0:T(8,128)(2,1)} %fusion), calls=%async_computation.1 | async-start | bytes 3670016 | tf_op jit(solution)/shard_map/all_to_all | solution.py:50
where the time goes:
time: 112 us
  blocking collectives  51.5 us (46%)
  waiting for transfers between devices  42.1 us (38%)
  matrix products  9.13 us (8%)
  starting transfers between devices  3.84 us (3%)
  local copies, waits for them, and re-layouts  2.92 us (3%)
  other arithmetic  1.94 us (2%)
    all_to_all x1, blocking collectives, shards(): lax.all_to_all(copies, ('node', 'ep'), split_axis=1, concat_axis=0, tiled...  51.5 us
    all_to_all x1, waiting for transfers between devices, shards(): lax.all_to_all(partial_value, ('node', 'ep'), split_axis=0, concat_axis=1...  42.1 us
    dot_general x1, matrix products, shards(): jnp.dot(inner_act, w_down, preferred_element_type=jnp.float32)  6.55 us
    all_to_all x1, starting transfers between devices, shards(): lax.all_to_all(partial_value, ('node', 'ep'), split_axis=0, concat_axis=1...  3.84 us
  transfers between devices with their start and end apart: 1, of which 1 were waited for; matrix products, arithmetic and copies ran while one was open for 0% of the time, Pallas kernels for 0%

commit v1 on v0

--- a/solution.py
+++ b/solution.py
@@ -1,11 +1,18 @@
+import functools
+
 import jax
 import jax.numpy as jnp
 from jax import lax
+from jax.experimental import pallas as pl
+from jax.experimental.pallas import tpu as pltpu
 from jax.sharding import PartitionSpec as P
 
+MESH = pl.DeviceIdType.MESH
 TOPK = 8
 SHARDS = 8
 SEND_CAP = 8
+SIDE = 2
+PIECES = 2
 
 
 def shards(activations, expert_ids, route_scores, capacity, w_gate, w_up, w_down):
@@ -58,6 +65,328 @@
     return mixed_out.astype(jnp.bfloat16)
 
 
+def chunk_of(width):
+    for size in (1024, 512, 256):
+        if width % size == 0:
+            return size
+    return 128
+
+
+def expert_kernel(
+    line, a_ref, wg_hbm, wu_hbm, wd_hbm, out_ref,
+    wg, wu, wd, gate_sum, up_sum, xb, core_in, part, side_in, up_in, down_in, stage,
+    w_sem, core_sem, up_sem, down_sem, side_sem, zrecv_sem, yrecv_sem,
+    p_side_sem, p_side_recv, p_up_sem, p_up_recv, p_down_sem, p_down_recv, last_sem, last_recv,
+):
+    node = lax.axis_index("node")
+    ep = lax.axis_index("ep")
+    z, y = ep // SIDE, ep % SIDE
+    other = 1 - y
+    rows, width = a_ref.shape[1], a_ref.shape[2]
+    piece = width // PIECES
+    to_core = {"node": 1 - node}
+    to_side = {"ep": z * SIDE + other}
+    to_up = {"ep": ep + SIDE}
+    to_down = {"ep": ep - SIDE}
+    has_up, has_down = z < line - 1, z > 0
+
+    loads = [
+        pltpu.make_async_copy(src, dst, w_sem.at[i])
+        for i, (src, dst) in enumerate(((wg_hbm, wg), (wu_hbm, wu), (wd_hbm, wd)))
+    ]
+    for load in loads:
+        load.start()
+
+    barrier = pltpu.get_barrier_semaphore()
+    pl.semaphore_signal(barrier, inc=1, device_id=to_core, device_id_type=MESH)
+    pl.semaphore_signal(barrier, inc=1, device_id=to_side, device_id_type=MESH)
+
+    @pl.when(has_up)
+    def _():
+        pl.semaphore_signal(barrier, inc=1, device_id=to_up, device_id_type=MESH)
+
+    @pl.when(has_down)
+    def _():
+        pl.semaphore_signal(barrier, inc=1, device_id=to_down, device_id_type=MESH)
+
+    pl.semaphore_wait(barrier, 2 + has_up.astype(jnp.int32) + has_down.astype(jnp.int32))
+
+    def cols(c):
+        return pl.ds(c * piece, piece)
+
+    def remote(src, dst, send, recv, where):
+        return pltpu.make_async_remote_copy(
+            src_ref=src, dst_ref=dst, send_sem=send, recv_sem=recv,
+            device_id=where, device_id_type=MESH,
+        )
+
+    def core_copy(c):
+        return remote(
+            a_ref.at[1 - node, :, cols(c)], core_in.at[:, cols(c)],
+            core_sem.at[0, c], core_sem.at[1, c], to_core,
+        )
+
+    def x_copy(o, c, send, recv, where):
+        ref = xb.at[o * SIDE + y, :, cols(c)]
+        return remote(ref, ref, send.at[o, c], recv.at[o, c], where)
+
+    def x_up(o, c):
+        return x_copy(o, c, up_sem, zrecv_sem, to_up)
+
+    def x_down(o, c):
+        return x_copy(o, c, down_sem, zrecv_sem, to_down)
+
+    def x_side(o, c):
+        return x_copy(o, c, side_sem, yrecv_sem, to_side)
+
+    for c in range(PIECES):
+        core_copy(c).start()
+    for c in range(PIECES):
+        core_copy(c).wait_recv()
+        xb[ep, :, cols(c)] = a_ref[node, :, cols(c)] + core_in[:, cols(c)]
+        pl.when(has_up)(lambda c=c: x_up(z, c).start())
+        pl.when(has_down)(lambda c=c: x_down(z, c).start())
+        x_side(z, c).start()
+
+    for d in range(1, line):
+        for c in range(PIECES):
+            @pl.when(z - d >= 0)
+            def _():
+                x_up(z - d, c).wait_recv()
+                pl.when(has_up)(lambda: x_up(z - d, c).start())
+                x_side(z - d, c).start()
+
+            @pl.when(z + d < line)
+            def _():
+                x_down(z + d, c).wait_recv()
+                pl.when(has_down)(lambda: x_down(z + d, c).start())
+                x_side(z + d, c).start()
+
+    for o in range(line):
+        for c in range(PIECES):
+            x_side(o, c).wait_recv()
+
+    count = xb.shape[0] * rows
+    loads[0].wait()
+    loads[1].wait()
+    gate_sum[...] = jnp.zeros_like(gate_sum)
+    up_sum[...] = jnp.zeros_like(up_sum)
+    step = chunk_of(width)
+
+    @pl.loop(0, width // step)
+    def _(k):
+        at = pl.ds(pl.multiple_of(k * step, step), step)
+        x = xb[:, :, at].reshape(count, step)
+        gate_sum[...] += jnp.dot(x, wg[at, :], preferred_element_type=jnp.float32)
+        up_sum[...] += jnp.dot(x, wu[at, :], preferred_element_type=jnp.float32)
+
+    gate = gate_sum[...]
+    inner = (gate / (1.0 + jnp.exp(-gate)) * up_sum[...]).astype(jnp.bfloat16)
+    loads[2].wait()
+    step = chunk_of(piece)
+
+    def p_side(t, c):
+        return remote(
+            part.at[t * SIDE + other, :, cols(c)], side_in.at[t, :, cols(c)],
+            p_side_sem.at[t, c], p_side_recv.at[t, c], to_side,
+        )
+
+    def p_up(t, c):
+        return remote(
+            stage.at[t, :, cols(c)], up_in.at[t, :, cols(c)],
+            p_up_sem.at[t, c], p_up_recv.at[t, c], to_up,
+        )
+
+    def p_down(t, c):
+        return remote(
+            stage.at[t, :, cols(c)], down_in.at[t, :, cols(c)],
+            p_down_sem.at[t, c], p_down_recv.at[t, c], to_down,
+        )
+
+    def last(c):
+        ref = out_ref.at[node, :, cols(c)]
+        return remote(ref, ref, last_sem.at[c], last_recv.at[c], to_core)
+
+    for c in range(PIECES):
+        @pl.loop(0, piece // step)
+        def _(k):
+            at = pl.ds(pl.multiple_of(c * piece + k * step, step), step)
+            value = jnp.dot(inner, wd[:, at], preferred_element_type=jnp.float32)
+            part[:, :, at] = value.astype(part.dtype).reshape(part.shape[0], rows, step)
+
+        for d in range(line - 1, 0, -1):
+            pl.when(z + d < line)(lambda: p_side(z + d, c).start())
+            pl.when(z - d >= 0)(lambda: p_side(z - d, c).start())
+        p_side(z, c).start()
+
+    def f32(ref, t, c):
+        return ref[t, :, cols(c)].astype(jnp.float32)
+
+    def here(t, c):
+        return f32(part, t * SIDE + y, c) + f32(side_in, t, c)
+
+    for c in range(PIECES):
+        for d in range(line - 1, 0, -1):
+            @pl.when(z + d < line)
+            def _():
+                t = z + d
+                p_side(t, c).wait_recv()
+
+                @pl.when(has_down)
+                def _():
+                    p_up(t, c).wait_recv()
+                    stage[t, :, cols(c)] = (here(t, c) + f32(up_in, t, c)).astype(stage.dtype)
+
+                @pl.when(z == 0)
+                def _():
+                    stage[t, :, cols(c)] = here(t, c).astype(stage.dtype)
+
+                p_up(t, c).start()
+
+            @pl.when(z - d >= 0)
+            def _():
+                t = z - d
+                p_side(t, c).wait_recv()
+
+                @pl.when(has_up)
+                def _():
+                    p_down(t, c).wait_recv()
+                    stage[t, :, cols(c)] = (here(t, c) + f32(down_in, t, c)).astype(stage.dtype)
+
+                @pl.when(z == line - 1)
+                def _():
+                    stage[t, :, cols(c)] = here(t, c).astype(stage.dtype)
+
+                p_down(t, c).start()
+
+        p_side(z, c).wait_recv()
+
+        @pl.when(has_down)
+        def _():
+            p_up(z, c).wait_recv()
+
+        @pl.when(has_up)
+        def _():
+            p_down(z, c).wait_recv()
+
+        @pl.when(has_down & has_up)
+        def _():
+            total = here(z, c) + f32(up_in, z, c) + f32(down_in, z, c)
+            out_ref[node, :, cols(c)] = total.astype(out_ref.dtype)
+
+        @pl.when(z == 0)
+        def _():
+            total = here(z, c) + f32(down_in, z, c)
+            out_ref[node, :, cols(c)] = total.astype(out_ref.dtype)
+
+        @pl.when(z == line - 1)
+        def _():
+            total = here(z, c) + f32(up_in, z, c)
+            out_ref[node, :, cols(c)] = total.astype(out_ref.dtype)
+
+        last(c).start()
+
+    for c in range(PIECES):
+        core_copy(c).wait_send()
+        x_side(z, c).wait_send()
+        pl.when(has_up)(lambda: x_up(z, c).wait_send())
+        pl.when(has_down)(lambda: x_down(z, c).wait_send())
+        p_side(z, c).wait_send()
+        for d in range(1, line):
+            @pl.when(z - d >= 0)
+            def _():
+                pl.when(has_up)(lambda: x_up(z - d, c).wait_send())
+                x_side(z - d, c).wait_send()
+                p_side(z - d, c).wait_send()
+                p_down(z - d, c).wait_send()
+
+            @pl.when(z + d < line)
+            def _():
+                pl.when(has_down)(lambda: x_down(z + d, c).wait_send())
+                x_side(z + d, c).wait_send()
+                p_side(z + d, c).wait_send()
+                p_up(z + d, c).wait_send()
+
+        last(c).wait_recv()
+        last(c).wait_send()
+
+
+def run_experts(rows_by_expert, w_gate, w_up, w_down):
+    experts, rows, width = rows_by_expert.shape
+    n_ep = lax.axis_size("ep")
+    line = n_ep // SIDE
+    hidden = w_gate.shape[1]
+    kind = rows_by_expert.dtype
+    count = n_ep * rows
+    vmem = pltpu.VMEM
+    sems = pltpu.SemaphoreType.DMA
+    flops = 6 * count * width * hidden
+    return pl.pallas_call(
+        functools.partial(expert_kernel, line),
+        out_shape=jax.ShapeDtypeStruct((experts, rows, width), kind),
+        in_specs=[pl.BlockSpec(memory_space=pltpu.VMEM)] + [pl.BlockSpec(memory_space=pl.ANY)] * 3,
+        out_specs=pl.BlockSpec(memory_space=pltpu.VMEM),
+        scratch_shapes=[
+            vmem(w_gate.shape, kind),
+            vmem(w_up.shape, kind),
+            vmem(w_down.shape, kind),
+            vmem((count, hidden), jnp.float32),
+            vmem((count, hidden), jnp.float32),
+            vmem((n_ep, rows, width), kind),
+            vmem((rows, width), kind),
+            vmem((n_ep, rows, width), kind),
+            vmem((line, rows, width), kind),
+            vmem((line, rows, width), kind),
+            vmem((line, rows, width), kind),
+            vmem((line, rows, width), kind),
+            sems((3,)),
+            sems((2, PIECES)),
+        ]
+        + [sems((line, PIECES))] * 11
+        + [sems((PIECES,))] * 2,
+        compiler_params=pltpu.CompilerParams(
+            collective_id=0, has_side_effects=True, vmem_limit_bytes=48 * 1024 * 1024
+        ),
+        cost_estimate=pl.CostEstimate(
+            flops=flops, bytes_accessed=6 * width * hidden, transcendentals=count * hidden
+        ),
+        name="routed_experts",
+    )(rows_by_expert, w_gate, w_up, w_down)
+
+
+def grid_shards(activations, expert_ids, route_scores, capacity, w_gate, w_up, w_down):
+    cores = lax.axis_size("node")
+    tok_rows, width = activations.shape
+    window = cores
+    route_weight = (2.5 * route_scores / jnp.sum(route_scores, axis=1, keepdims=True)).astype(
+        jnp.bfloat16
+    )
+    flat_ids = expert_ids.reshape(-1)
+    expert_iota = jnp.arange(window, dtype=jnp.int32)
+    onehot = (flat_ids[:, None] == expert_iota[None, :]).astype(jnp.int32)
+    running = jnp.cumsum(onehot, axis=0)
+    ranking = jnp.sum(onehot * running, axis=1) - 1
+    limits = jnp.sum(onehot * capacity[:window][None, :], axis=1)
+    is_live = (flat_ids < window) & (ranking < limits)
+    mine = lax.axis_index("node") * SEND_CAP
+    slots = cores * SEND_CAP
+    slot_index = jnp.where(is_live, flat_ids * slots + mine + ranking, -1).reshape(tok_rows, TOPK)
+    positions = jnp.arange(window * slots, dtype=jnp.int32)
+    matches = slot_index[:, :, None] == positions[None, None, :]
+    select = jnp.any(matches, axis=1).astype(jnp.bfloat16)
+    combine_w = jnp.sum(
+        jnp.where(matches, route_weight[:, :, None].astype(jnp.float32), 0.0), axis=1
+    ).astype(jnp.bfloat16)
+    sent = lax.dot_general(
+        select, activations, (((0,), (0,)), ((), ())), preferred_element_type=jnp.float32
+    ).astype(jnp.bfloat16)
+    expert_out = run_experts(sent.reshape(window, slots, width), w_gate, w_up, w_down)
+    mixed_out = jnp.dot(
+        combine_w, expert_out.reshape(window * slots, width), preferred_element_type=jnp.float32
+    )
+    return mixed_out.astype(jnp.bfloat16)
+
+
 def solution(mesh):
     placed = (
         P(("rep", "node", "ep"), None),
@@ -68,8 +397,9 @@
         P(None, ("node", "ep")),
         P(("node", "ep"), None),
     )
+    fits = mesh.shape["ep"] == SHARDS and mesh.shape["node"] == 2
     return jax.shard_map(
-        shards,
+        grid_shards if fits else shards,
         mesh=mesh,
         in_specs=placed,
         out_specs=P(("rep", "node", "ep"), None),

time: 112 us -> 71.1 us (0.63)
  Pallas kernels: 0 us -> 61.4 us
  blocking collectives: 51.5 us -> 0 us
  waiting for transfers between devices: 42.1 us -> 0 us
  matrix products: 9.13 us -> 1.93 us
  starting transfers between devices: 3.84 us -> 0 us
  local copies, waits for them, and re-layouts: 2.92 us -> 4.28 us
  other arithmetic: 1.94 us -> 3.1 us
    pallas_call x0 -> x1, Pallas kernels: none -> 61.4 us  [run_experts(): pl.pallas_call(functools.partial(expert_kernel, line), out_shape=jax.Shap...]
    all_to_all x1 -> x0, blocking collectives: 51.5 us -> none  [shards(): lax.all_to_all(copies, ('node', 'ep'), split_axis=1, concat_axis=0, tiled...]
    all_to_all x1 -> x0, waiting for transfers between devices: 42.1 us -> none  [shards(): lax.all_to_all(partial_value, ('node', 'ep'), split_axis=0, concat_axis=1...]
    dot_general x4 -> x2, matrix products: 9.13 us -> 1.93 us  [the longest x1 1.62 us: grid_shards(): jnp.dot(combine_w, expert_out.reshape(window * slots, width), preferred_e...]
    all_to_all x1 -> x0, starting transfers between devices: 3.84 us -> none  [shards(): lax.all_to_all(partial_value, ('node', 'ep'), split_axis=0, concat_axis=1...]
    unnamed x7 -> x5, local copies, waits for them, and re-layouts: 0.9 us -> 2.82 us
  transfers between devices with their start and end apart: 1 -> 0, of which waited for: 1 -> 0; matrix products, arithmetic and copies ran while one was open for 0% -> 0% of each run, Pallas kernels for 0% -> 0%
where the time goes in v1:
time: 71.1 us; the launch traced here: 70.8 us
  Pallas kernels  61.4 us (86%)
  local copies, waits for them, and re-layouts  4.28 us (6%)
  other arithmetic  3.1 us (4%)
  matrix products  1.93 us (3%)
    pallas_call x1, Pallas kernels, run_experts(): pl.pallas_call(functools.partial(expert_kernel, line), out_shape=jax.Shap...  61.4 us
    unnamed x5, local copies, waits for them, and re-layouts  2.82 us
    dot_general x1, matrix products, grid_shards(): jnp.dot(combine_w, expert_out.reshape(window * slots, width), preferred_e...  1.62 us

profile of v1, /device:TPU:0, one launch (start us, length us, event | category | flops | bytes accessed | tf_op | source)
XLA Modules:
  0.0 70.8 jit_solution(4027558682726896008)
XLA Ops:
  0.0 0.0 copy-start
  0.0 0.8 %slice.11 = s32[2]{0:T(128)S(1)} slice(s32[256]{0:T(256)} %param.10), slice={[0:2]} | slice | bytes 16 | tf_op jit(solution)/shard_map/slice | solution.py:369
  0.8 0.7 reduce_sum.41
  1.5 0.7 fusion.5
  2.2 0.8 %copy.26 = s32[96,8]{1,0:T(8,128)S(1)} copy(s32[96,8]{0,1:T(8,128)} %param.8) | data formatting | bytes 6144 | tf_op args[1]
  3.0 0.1 eq.42
  3.1 0.1 eq.38
  3.2 0.6 reduce-window.6
  3.7 0.2 slice_reduce_fusion
  4.0 0.2 reduce-window.9
  4.1 0.1 add_bitcast_fusion
  4.2 0.1 select_reduce_fusion.1
  4.3 0.1 sub.7
  4.4 0.1 copy.28
  4.5 0.1 reduce_sum.40
  4.6 0.1 copy.29
  4.6 0.7 %add_select_fusion = s32[96,8]{0,1:T(8,128)S(1)} fusion(s32[96,8]{0,1:T(8,128)S(1)} %copy.28, s32[96,8]{0,1:T(8,128)} %param.8, s32[96,8]{0,1:T(8,128)S(1)} %copy.29, s32[]{:T(128)S(6)} %mul.33), kind=kLoop, calls=%fused_computation.16 | loop fusion | flops 5376 | bytes 12292 | tf_op jit(solution)/shard_map/jit(_where)/select_n | solution.py:373
  5.4 0.0 copy-done
  5.4 0.3 convolution_convert_fusion.1
  5.7 0.0 copy-start.1
  5.7 2.0 %copy-done.1 = bf16[7168,256]{1,0:T(8,128)(2,1)S(1)} copy-done((bf16[7168,256]{1,0:T(8,128)(2,1)S(1)}, bf16[7168,256]{1,0:T(8,128)(2,1)}, u32[]{:S(2)}) %copy-start.1) | copy-done | bytes 3670040
  7.8 61.4 %routed_experts.1 = bf16[2,16,7168]{2,1,0:T(8,128)(2,1)S(1)} custom-call(bf16[2,16,7168]{2,1,0:T(8,128)(2,1)S(1)} %bitcast.22, bf16[7168,256]{1,0:T(8,128)(2,1)S(1)} %copy-done.1, bf16[7168,256]{1,0:T(8,128)(2,1)} %wu_hbm.1, bf16[256,7168]{1,0:T(8,128)(2,1)} %wd_hbm.1), custom_call_target="tpu_custom_call" | custom-call | flops 1409286144 | bytes 11010048 | tf_op jit(solution)/shard_map/routed_experts/pallas_call | solution.py:324
  69.2 1.6 %convolution_convert_fusion = bf16[96,7168]{1,0:T(8,128)(2,1)} fusion(bf16[32,7168]{1,0:T(8,128)(2,1)S(1)} %bitcast.21, bf16[96,32]{0,1:T(8,128)(2,1)S(1)} %select_reduce_fusion), kind=kOutput, calls=%fused_computation | convolution fusion | flops 44728320 | bytes 1841152 | tf_op jit(solution)/shard_map/dot_general | solution.py:384
  (4 shorter events, 0.1 us)
Async XLA Ops:
  0.0 5.4 %copy-start = (bf16[96,7168]{1,0:T(8,128)(2,1)S(1)}, bf16[96,7168]{1,0:T(8,128)(2,1)}, u32[]{:S(2)}) copy-start(bf16[96,7168]{1,0:T(8,128)(2,1)} %param.7) | copy-start | bytes 4128772
  5.7 2.0 %copy-start.1 = (bf16[7168,256]{1,0:T(8,128)(2,1)S(1)}, bf16[7168,256]{1,0:T(8,128)(2,1)}, u32[]{:S(2)}) copy-start(bf16[7168,256]{1,0:T(8,128)(2,1)} %wg_hbm.1) | copy-start | bytes 11010052

commit v2 on v0

--- a/solution.py
+++ b/solution.py
@@ -1,11 +1,17 @@
+import functools
+
 import jax
 import jax.numpy as jnp
 from jax import lax
+from jax.experimental import pallas as pl
+from jax.experimental.pallas import tpu as pltpu
 from jax.sharding import PartitionSpec as P
 
+MESH = pl.DeviceIdType.MESH
 TOPK = 8
 SHARDS = 8
 SEND_CAP = 8
+SIDE = 2
 
 
 def shards(activations, expert_ids, route_scores, capacity, w_gate, w_up, w_down):
@@ -58,6 +64,416 @@
     return mixed_out.astype(jnp.bfloat16)
 
 
+def piece_of(width):
+    for size in (1024, 512, 256):
+        if width % size == 0:
+            return size
+    return 128
+
+
+def select_rows(node, experts, ids_ref, score_ref, cap_ref):
+    ids, scores = ids_ref[...], score_ref[...]
+    tokens = ids.shape[0]
+    slots = experts * SEND_CAP
+    weight = (2.5 * scores / jnp.sum(scores, axis=1, keepdims=True)).astype(jnp.bfloat16)
+    weight = weight.astype(jnp.float32)
+    column = lax.broadcasted_iota(jnp.int32, (tokens, experts * slots), 1)
+    rank_of = column % slots - node * SEND_CAP
+    hit = jnp.zeros(column.shape, jnp.float32)
+    hit_weight = jnp.zeros(column.shape, jnp.float32)
+    limit = jnp.zeros(column.shape, jnp.int32)
+    for e in range(experts):
+        named = ids == e
+        here = column // slots == e
+        any_named = jnp.sum(jnp.where(named, 1.0, 0.0), axis=1, keepdims=True)
+        its_weight = jnp.sum(jnp.where(named, weight, 0.0), axis=1, keepdims=True)
+        hit = jnp.where(here, any_named, hit)
+        hit_weight = jnp.where(here, its_weight, hit_weight)
+        limit = jnp.where(here, cap_ref[e], limit)
+    before = lax.broadcasted_iota(jnp.int32, (tokens, tokens), 0) > lax.broadcasted_iota(
+        jnp.int32, (tokens, tokens), 1
+    )
+    rank = jnp.dot(
+        jnp.where(before, 1.0, 0.0).astype(jnp.bfloat16),
+        hit.astype(jnp.bfloat16),
+        preferred_element_type=jnp.float32,
+    ).astype(jnp.int32)
+    live = (hit > 0.5) & (rank == rank_of) & (rank_of >= 0) & (rank_of < SEND_CAP) & (rank < limit)
+    select = jnp.where(live, 1.0, 0.0).astype(jnp.bfloat16)
+    return select, jnp.where(live, hit_weight, 0.0).astype(jnp.bfloat16)
+
+
+def expert_kernel(
+    line, cap_ref, ids_ref, score_ref, act_ref, wg_hbm, wu_hbm, wd_hbm, out_ref, mix_ref,
+    wg, wu, wd, gate_sum, up_sum, sent, xb, core_in, part,
+    side_in, up_in, down_in, stage, far_up, far_down, far_stage,
+    w_sem, core_sem, up_sem, down_sem, side_sem, zrecv_sem, yrecv_sem,
+    p_side_sem, p_side_recv, p_up_sem, p_up_recv, p_down_sem, p_down_recv, last_sem, last_recv,
+    far_sem,
+):
+    node = lax.axis_index("node")
+    ep = lax.axis_index("ep")
+    z, y = ep // SIDE, ep % SIDE
+    other = 1 - y
+    experts, rows, width = sent.shape
+    piece = far_stage.shape[2]
+    pieces = width // piece
+    to_core = {"node": 1 - node}
+    to_side = {"ep": z * SIDE + other}
+    to_up = {"ep": ep + SIDE}
+    to_down = {"ep": ep - SIDE}
+    has_up, has_down = z < line - 1, z > 0
+
+    loads = [
+        pltpu.make_async_copy(src, dst, w_sem.at[i])
+        for i, (src, dst) in enumerate(((wg_hbm, wg), (wu_hbm, wu), (wd_hbm, wd)))
+    ]
+    for load in loads:
+        load.start()
+
+    barrier = pltpu.get_barrier_semaphore()
+    pl.semaphore_signal(barrier, inc=1, device_id=to_core, device_id_type=MESH)
+    pl.semaphore_signal(barrier, inc=1, device_id=to_side, device_id_type=MESH)
+
+    @pl.when(has_up)
+    def _():
+        pl.semaphore_signal(barrier, inc=1, device_id=to_up, device_id_type=MESH)
+
+    @pl.when(has_down)
+    def _():
+        pl.semaphore_signal(barrier, inc=1, device_id=to_down, device_id_type=MESH)
+
+    def cols(c):
+        return pl.ds(c * piece, piece)
+
+    def remote(src, dst, send, recv, where):
+        return pltpu.make_async_remote_copy(
+            src_ref=src, dst_ref=dst, send_sem=send, recv_sem=recv,
+            device_id=where, device_id_type=MESH,
+        )
+
+    def core_copy(c):
+        return remote(
+            sent.at[1 - node, :, cols(c)], core_in.at[:, cols(c)],
+            core_sem.at[0, c], core_sem.at[1, c], to_core,
+        )
+
+    def x_copy(o, c, send, recv, where):
+        ref = xb.at[o * SIDE + y, :, cols(c)]
+        return remote(ref, ref, send.at[o, c], recv.at[o, c], where)
+
+    def x_up(o, c):
+        return x_copy(o, c, up_sem, zrecv_sem, to_up)
+
+    def x_down(o, c):
+        return x_copy(o, c, down_sem, zrecv_sem, to_down)
+
+    def x_side(o, c):
+        return x_copy(o, c, side_sem, yrecv_sem, to_side)
+
+    def far(o, i, where):
+        ref = xb.at[o * SIDE + other, :, cols(0)]
+        return remote(ref, ref, far_sem.at[i, o], far_sem.at[2, o], where)
+
+    def x_far_up(o):
+        return far(o, 0, to_up)
+
+    def x_far_down(o):
+        return far(o, 1, to_down)
+
+    select, mix = select_rows(node, experts, ids_ref, score_ref, cap_ref)
+    mix_ref[...] = mix
+    for c in range(pieces):
+        taken = lax.dot_general(
+            select, act_ref[:, cols(c)], (((0,), (0,)), ((), ())),
+            preferred_element_type=jnp.float32,
+        )
+        sent[:, :, cols(c)] = taken.astype(sent.dtype).reshape(experts, rows, piece)
+        if c == 0:
+            pl.semaphore_wait(barrier, 2 + has_up.astype(jnp.int32) + has_down.astype(jnp.int32))
+        core_copy(c).start()
+    for c in range(pieces):
+        core_copy(c).wait_recv()
+        xb[ep, :, cols(c)] = sent[node, :, cols(c)] + core_in[:, cols(c)]
+        x_side(z, c).start()
+        pl.when(has_up)(lambda: x_up(z, c).start())
+        pl.when(has_down)(lambda: x_down(z, c).start())
+
+    x_side(z, 0).wait_recv()
+    pl.when(has_up)(lambda: x_far_up(z).start())
+    pl.when(has_down)(lambda: x_far_down(z).start())
+
+    for d in range(1, line):
+        for c in range(pieces):
+            @pl.when(z - d >= 0)
+            def _():
+                x_up(z - d, c).wait_recv()
+                pl.when(has_up)(lambda: x_up(z - d, c).start())
+                if c > 0:
+                    x_side(z - d, c).start()
+
+            @pl.when(z + d < line)
+            def _():
+                x_down(z + d, c).wait_recv()
+                pl.when(has_down)(lambda: x_down(z + d, c).start())
+                if c > 0:
+                    x_side(z + d, c).start()
+
+        @pl.when(z - d >= 0)
+        def _():
+            x_far_up(z - d).wait_recv()
+            pl.when(has_up)(lambda: x_far_up(z - d).start())
+
+        @pl.when(z + d < line)
+        def _():
+            x_far_down(z + d).wait_recv()
+            pl.when(has_down)(lambda: x_far_down(z + d).start())
+
+    count = xb.shape[0] * rows
+    loads[0].wait()
+    loads[1].wait()
+    for c in range(pieces):
+        if c > 0:
+            for o in range(line):
+                x_side(o, c).wait_recv()
+        x = xb[:, :, cols(c)].reshape(count, piece)
+        gate_part = jnp.dot(x, wg[cols(c), :], preferred_element_type=jnp.float32)
+        up_part = jnp.dot(x, wu[cols(c), :], preferred_element_type=jnp.float32)
+        if c == 0:
+            gate_sum[...] = gate_part
+            up_sum[...] = up_part
+        else:
+            gate_sum[...] += gate_part
+            up_sum[...] += up_part
+
+    gate = gate_sum[...]
+    inner = (gate / (1.0 + jnp.exp(-gate)) * up_sum[...]).astype(jnp.bfloat16)
+    loads[2].wait()
+
+    def p_side(t, c):
+        src = far_stage.at[t] if c == 0 else part.at[t * SIDE + other, :, cols(c)]
+        return remote(
+            src, side_in.at[t, :, cols(c)],
+            p_side_sem.at[t, c], p_side_recv.at[t, c], to_side,
+        )
+
+    def p_up(t, c):
+        return remote(
+            stage.at[t, :, cols(c)], up_in.at[t, :, cols(c)],
+            p_up_sem.at[t, c], p_up_recv.at[t, c], to_up,
+        )
+
+    def p_down(t, c):
+        return remote(
+            stage.at[t, :, cols(c)], down_in.at[t, :, cols(c)],
+            p_down_sem.at[t, c], p_down_recv.at[t, c], to_down,
+        )
+
+    def p_far_up(t):
+        return remote(far_stage.at[t], far_up.at[t], far_sem.at[3, t], far_sem.at[4, t], to_up)
+
+    def p_far_down(t):
+        return remote(far_stage.at[t], far_down.at[t], far_sem.at[5, t], far_sem.at[6, t], to_down)
+
+    def last(c):
+        ref = out_ref.at[node, :, cols(c)]
+        return remote(ref, ref, last_sem.at[c], last_recv.at[c], to_core)
+
+    def at_distance(d, act):
+        pl.when(z + d < line)(lambda: act(z + d, True))
+        pl.when(z - d >= 0)(lambda: act(z - d, False))
+
+    def f32(ref, t, c):
+        return ref[t, :, cols(c)].astype(jnp.float32)
+
+    def here(t, c):
+        own = f32(part, t * SIDE + y, c)
+        return own if c == 0 else own + f32(side_in, t, c)
+
+    def there(t):
+        return f32(part, t * SIDE + other, 0)
+
+    def pass_on(t, c, upward):
+        if c > 0:
+            p_side(t, c).wait_recv()
+        copy, arrived = (p_up, up_in) if upward else (p_down, down_in)
+        more, end = (has_down, z == 0) if upward else (has_up, z == line - 1)
+
+        @pl.when(more)
+        def _():
+            copy(t, c).wait_recv()
+            stage[t, :, cols(c)] = (here(t, c) + f32(arrived, t, c)).astype(stage.dtype)
+
+        @pl.when(end)
+        def _():
+            stage[t, :, cols(c)] = here(t, c).astype(stage.dtype)
+
+        copy(t, c).start()
+
+    def pass_far(t, upward):
+        copy, arrived = (p_far_up, far_up) if upward else (p_far_down, far_down)
+        more, end = (has_down, z == 0) if upward else (has_up, z == line - 1)
+
+        @pl.when(more)
+        def _():
+            copy(t).wait_recv()
+            far_stage[t] = (there(t) + arrived[t].astype(jnp.float32)).astype(far_stage.dtype)
+
+        @pl.when(end)
+        def _():
+            far_stage[t] = there(t).astype(far_stage.dtype)
+
+        copy(t).start()
+
+    order = list(range(1, pieces)) + [0]
+    for c in order:
+        value = jnp.dot(inner, wd[:, cols(c)], preferred_element_type=jnp.float32)
+        part[:, :, cols(c)] = value.astype(part.dtype).reshape(part.shape[0], rows, piece)
+        if c > 0:
+            at_distance(line - 1, lambda t, upward: p_side(t, c).start())
+            if line > 2:
+                at_distance(line - 2, lambda t, upward: p_side(t, c).start())
+    for d in range(line - 3, 0, -1):
+        for c in range(1, pieces):
+            at_distance(d, lambda t, upward: p_side(t, c).start())
+    for c in range(1, pieces):
+        p_side(z, c).start()
+
+    for d in range(line - 1, 0, -1):
+        at_distance(d, lambda t, upward: pass_on(t, 0, upward))
+        at_distance(d, pass_far)
+        for c in range(1, pieces):
+            at_distance(d, lambda t, upward: pass_on(t, c, upward))
+
+    def far_sum(with_up, with_down):
+        total = there(z)
+        if with_up:
+            total = total + far_up[z].astype(jnp.float32)
+        if with_down:
+            total = total + far_down[z].astype(jnp.float32)
+        far_stage[z] = total.astype(far_stage.dtype)
+
+    def near_sum(c, with_up, with_down):
+        total = f32(part, ep, c) + f32(side_in, z, c)
+        if with_up:
+            total = total + f32(up_in, z, c)
+        if with_down:
+            total = total + f32(down_in, z, c)
+        out_ref[node, :, cols(c)] = total.astype(out_ref.dtype)
+
+    def by_place(add):
+        pl.when(has_down & has_up)(lambda: add(True, True))
+        pl.when(z == 0)(lambda: add(False, True))
+        pl.when(z == line - 1)(lambda: add(True, False))
+
+    pl.when(has_down)(lambda: p_far_up(z).wait_recv())
+    pl.when(has_up)(lambda: p_far_down(z).wait_recv())
+    by_place(far_sum)
+    p_side(z, 0).start()
+    for c in order:
+        p_side(z, c).wait_recv()
+        pl.when(has_down)(lambda: p_up(z, c).wait_recv())
+        pl.when(has_up)(lambda: p_down(z, c).wait_recv())
+        by_place(lambda with_up, with_down: near_sum(c, with_up, with_down))
+        last(c).start()
+
+    def done_far(t, upward):
+        pl.when(has_down if upward else has_up)(
+            lambda: (x_far_down if upward else x_far_up)(t).wait_send()
+        )
+        (p_far_up if upward else p_far_down)(t).wait_send()
+
+    def done(t, c, upward):
+        pl.when(has_down if upward else has_up)(
+            lambda: (x_down if upward else x_up)(t, c).wait_send()
+        )
+        if c > 0:
+            x_side(t, c).wait_send()
+            p_side(t, c).wait_send()
+        (p_up if upward else p_down)(t, c).wait_send()
+
+    pl.when(has_up)(lambda: x_far_up(z).wait_send())
+    pl.when(has_down)(lambda: x_far_down(z).wait_send())
+    for d in range(1, line):
+        at_distance(d, done_far)
+    for c in range(pieces):
+        core_copy(c).wait_send()
+        x_side(z, c).wait_send()
+        pl.when(has_up)(lambda: x_up(z, c).wait_send())
+        pl.when(has_down)(lambda: x_down(z, c).wait_send())
+        p_side(z, c).wait_send()
+        for d in range(1, line):
+            at_distance(d, lambda t, upward: done(t, c, upward))
+    for c in order:
+        last(c).wait_recv()
+        last(c).wait_send()
+
+
+def run_experts(activations, expert_ids, route_scores, capacity, w_gate, w_up, w_down):
+    experts = lax.axis_size("node")
+    n_ep = lax.axis_size("ep")
+    tokens, width = activations.shape
+    rows = experts * SEND_CAP
+    line = n_ep // SIDE
+    hidden = w_gate.shape[1]
+    kind = activations.dtype
+    count = n_ep * rows
+    piece = piece_of(width)
+    pieces = width // piece
+    vmem = pltpu.VMEM
+    sems = pltpu.SemaphoreType.DMA
+    here = pl.BlockSpec(memory_space=pltpu.VMEM)
+    return pl.pallas_call(
+        functools.partial(expert_kernel, line),
+        out_shape=(
+            jax.ShapeDtypeStruct((experts, rows, width), kind),
+            jax.ShapeDtypeStruct((tokens, experts * rows), jnp.bfloat16),
+        ),
+        in_specs=[pl.BlockSpec(memory_space=pltpu.SMEM)]
+        + [here] * 3
+        + [pl.BlockSpec(memory_space=pl.ANY)] * 3,
+        out_specs=(here, here),
+        scratch_shapes=[
+            vmem(w_gate.shape, kind),
+            vmem(w_up.shape, kind),
+            vmem(w_down.shape, kind),
+            vmem((count, hidden), jnp.float32),
+            vmem((count, hidden), jnp.float32),
+            vmem((experts, rows, width), kind),
+            vmem((n_ep, rows, width), kind),
+            vmem((rows, width), kind),
+            vmem((n_ep, rows, width), kind),
+        ]
+        + [vmem((line, rows, width), kind)] * 4
+        + [vmem((line, rows, piece), kind)] * 3
+        + [sems((3,)), sems((2, pieces))]
+        + [sems((line, pieces))] * 11
+        + [sems((pieces,))] * 2
+        + [sems((7, line))],
+        compiler_params=pltpu.CompilerParams(
+            collective_id=0, has_side_effects=True, vmem_limit_bytes=48 * 1024 * 1024
+        ),
+        cost_estimate=pl.CostEstimate(
+            flops=6 * count * width * hidden,
+            bytes_accessed=6 * width * hidden,
+            transcendentals=count * hidden,
+        ),
+        name="routed_experts",
+    )(capacity, expert_ids, route_scores, activations, w_gate, w_up, w_down)
+
+
+def grid_shards(activations, expert_ids, route_scores, capacity, w_gate, w_up, w_down):
+    expert_out, combine_w = run_experts(
+        activations, expert_ids, route_scores, capacity, w_gate, w_up, w_down
+    )
+    mixed_out = jnp.dot(
+        combine_w,
+        expert_out.reshape(-1, expert_out.shape[2]),
+        preferred_element_type=jnp.float32,
+    )
+    return mixed_out.astype(jnp.bfloat16)
+
+
 def solution(mesh):
     placed = (
         P(("rep", "node", "ep"), None),
@@ -68,8 +484,9 @@
         P(None, ("node", "ep")),
         P(("node", "ep"), None),
     )
+    fits = mesh.shape["ep"] == SHARDS and mesh.shape["node"] == 2
     return jax.shard_map(
-        shards,
+        grid_shards if fits else shards,
         mesh=mesh,
         in_specs=placed,
         out_specs=P(("rep", "node", "ep"), None),

time: 112 us -> 61 us (0.54)
  Pallas kernels: 0 us -> 53.5 us
  blocking collectives: 51.5 us -> 0 us
  waiting for transfers between devices: 42.1 us -> 0 us
  matrix products: 9.13 us -> 1.57 us
  starting transfers between devices: 3.84 us -> 0 us
  local copies, waits for them, and re-layouts: 2.92 us -> 5.61 us
  other arithmetic: 1.94 us -> 0 us
    pallas_call x0 -> x1, Pallas kernels: none -> 53.5 us  [run_experts(): pl.pallas_call(functools.partial(expert_kernel, line), out_shape=(jax.Sha...]
    all_to_all x1 -> x0, blocking collectives: 51.5 us -> none  [shards(): lax.all_to_all(copies, ('node', 'ep'), split_axis=1, concat_axis=0, tiled...]
    all_to_all x1 -> x0, waiting for transfers between devices: 42.1 us -> none  [shards(): lax.all_to_all(partial_value, ('node', 'ep'), split_axis=0, concat_axis=1...]
    dot_general x4 -> x1, matrix products: 9.13 us -> 1.57 us  [grid_shards(): jnp.dot(combine_w, expert_out.reshape(-1, expert_out.shape[2]), preferred...]
    unnamed x7 -> x8, local copies, waits for them, and re-layouts: 0.9 us -> 5.61 us
    all_to_all x1 -> x0, starting transfers between devices: 3.84 us -> none  [shards(): lax.all_to_all(partial_value, ('node', 'ep'), split_axis=0, concat_axis=1...]
  transfers between devices with their start and end apart: 1 -> 0, of which waited for: 1 -> 0; matrix products, arithmetic and copies ran while one was open for 0% -> 0% of each run, Pallas kernels for 0% -> 0%
where the time goes in v2:
time: 61 us; the launch traced here: 60.7 us
  Pallas kernels  53.5 us (88%)
  local copies, waits for them, and re-layouts  5.61 us (9%)
  matrix products  1.57 us (3%)
    pallas_call x1, Pallas kernels, run_experts(): pl.pallas_call(functools.partial(expert_kernel, line), out_shape=(jax.Sha...  53.5 us
    unnamed x8, local copies, waits for them, and re-layouts  5.61 us
    dot_general x1, matrix products, grid_shards(): jnp.dot(combine_w, expert_out.reshape(-1, expert_out.shape[2]), preferred...  1.57 us

profile of v2, /device:TPU:0, one launch (start us, length us, event | category | flops | bytes accessed | tf_op | source)
XLA Modules:
  0.0 60.7 jit_solution(10621460632402640481)
XLA Ops:
  0.0 0.8 %copy.8.ids_ref = s32[96,8]{1,0:T(8,128)S(1)} copy(s32[96,8]{0,1:T(8,128)} %param.8) | data formatting | bytes 6144 | tf_op args[1]
  0.8 0.8 %copy.9.score_ref = f32[96,8]{1,0:T(8,128)S(1)} copy(f32[96,8]{0,1:T(8,128)} %param.9) | data formatting | bytes 6144 | tf_op args[2]
  1.6 0.0 copy-start
  1.6 2.0 %copy-done = bf16[7168,256]{1,0:T(8,128)(2,1)S(1)} copy-done((bf16[7168,256]{1,0:T(8,128)(2,1)S(1)}, bf16[7168,256]{1,0:T(8,128)(2,1)}, u32[]{:S(2)}) %copy-start) | copy-done | bytes 3670040
  3.6 0.0 copy-start.1
  3.6 1.3 %copy-done.1 = bf16[96,7168]{1,0:T(8,128)(2,1)S(1)} copy-done((bf16[96,7168]{1,0:T(8,128)(2,1)S(1)}, bf16[96,7168]{1,0:T(8,128)(2,1)}, u32[]{:S(2)}) %copy-start.1) | copy-done | bytes 1376280
  4.9 0.0 copy-start.2
  4.9 0.7 %copy-done.2 = s32[256]{0:T(256)S(1)} copy-done((s32[256]{0:T(256)S(1)}, s32[256]{0:T(256)}, u32[]{:S(2)}) %copy-start.2) | copy-done | bytes 1048
  5.6 53.5 %routed_experts.1 = (bf16[2,16,7168]{2,1,0:T(8,128)(2,1)S(1)}, bf16[96,32]{1,0:T(8,128)(2,1)S(1)}) custom-call(s32[256]{0:T(256)S(1)} %copy-done.2, s32[96,8]{1,0:T(8,128)S(1)} %copy.8.ids_ref, f32[96,8]{1,0:T(8,128)S(1)} %copy.9.score_ref, bf16[96,7168]{1,0:T(8,128)(2,1)S(1)} %copy-done.1, bf16[7168,256]{1,0:T(8,128)(2,1)S(1)} %copy-done, ...), custom_call_target="tpu_custom_call" | custom-call | flops 1409286144 | bytes 11010048 | tf_op jit(solution)/shard_map/routed_experts/pallas_call | solution.py:426
  59.2 1.6 %convolution_convert_fusion = bf16[96,7168]{1,0:T(8,128)(2,1)} fusion(bf16[96,32]{1,0:T(8,128)(2,1)S(1)} %get-tuple-element.7, bf16[32,7168]{1,0:T(8,128)(2,1)S(1)} %bitcast.3), kind=kOutput, calls=%fused_computation | convolution fusion | flops 44728320 | bytes 1841152 | tf_op jit(solution)/shard_map/dot_general | solution.py:469
Async XLA Ops:
  1.6 2.0 %copy-start = (bf16[7168,256]{1,0:T(8,128)(2,1)S(1)}, bf16[7168,256]{1,0:T(8,128)(2,1)}, u32[]{:S(2)}) copy-start(bf16[7168,256]{1,0:T(8,128)(2,1)} %wg_hbm.1) | copy-start | bytes 11010052
  3.6 1.3 %copy-start.1 = (bf16[96,7168]{1,0:T(8,128)(2,1)S(1)}, bf16[96,7168]{1,0:T(8,128)(2,1)}, u32[]{:S(2)}) copy-start(bf16[96,7168]{1,0:T(8,128)(2,1)} %act_ref.1) | copy-start | bytes 4128772
  4.9 0.7 %copy-start.2 = (s32[256]{0:T(256)S(1)}, s32[256]{0:T(256)}, u32[]{:S(2)}) copy-start(s32[256]{0:T(256)} %cap_ref.1) | copy-start | bytes 3076

commit v3 on v2

--- a/solution.py
+++ b/solution.py
@@ -73,29 +73,29 @@
 
 def select_rows(node, experts, ids_ref, score_ref, cap_ref):
     ids, scores = ids_ref[...], score_ref[...]
-    tokens = ids.shape[0]
+    tokens = ids.shape[1]
     slots = experts * SEND_CAP
-    weight = (2.5 * scores / jnp.sum(scores, axis=1, keepdims=True)).astype(jnp.bfloat16)
+    weight = (2.5 * scores / jnp.sum(scores, axis=0, keepdims=True)).astype(jnp.bfloat16)
     weight = weight.astype(jnp.float32)
-    column = lax.broadcasted_iota(jnp.int32, (tokens, experts * slots), 1)
-    rank_of = column % slots - node * SEND_CAP
-    hit = jnp.zeros(column.shape, jnp.float32)
-    hit_weight = jnp.zeros(column.shape, jnp.float32)
-    limit = jnp.zeros(column.shape, jnp.int32)
+    line = lax.broadcasted_iota(jnp.int32, (experts * slots, tokens), 0)
+    rank_of = line % slots - node * SEND_CAP
+    hit = jnp.zeros(line.shape, jnp.float32)
+    hit_weight = jnp.zeros(line.shape, jnp.float32)
+    limit = jnp.zeros(line.shape, jnp.int32)
     for e in range(experts):
         named = ids == e
-        here = column // slots == e
-        any_named = jnp.sum(jnp.where(named, 1.0, 0.0), axis=1, keepdims=True)
-        its_weight = jnp.sum(jnp.where(named, weight, 0.0), axis=1, keepdims=True)
+        here = line // slots == e
+        any_named = jnp.sum(jnp.where(named, 1.0, 0.0), axis=0, keepdims=True)
+        its_weight = jnp.sum(jnp.where(named, weight, 0.0), axis=0, keepdims=True)
         hit = jnp.where(here, any_named, hit)
         hit_weight = jnp.where(here, its_weight, hit_weight)
         limit = jnp.where(here, cap_ref[e], limit)
-    before = lax.broadcasted_iota(jnp.int32, (tokens, tokens), 0) > lax.broadcasted_iota(
+    before = lax.broadcasted_iota(jnp.int32, (tokens, tokens), 0) < lax.broadcasted_iota(
         jnp.int32, (tokens, tokens), 1
     )
     rank = jnp.dot(
+        hit.astype(jnp.bfloat16),
         jnp.where(before, 1.0, 0.0).astype(jnp.bfloat16),
-        hit.astype(jnp.bfloat16),
         preferred_element_type=jnp.float32,
     ).astype(jnp.int32)
     live = (hit > 0.5) & (rank == rank_of) & (rank_of >= 0) & (rank_of < SEND_CAP) & (rank < limit)
@@ -104,12 +104,12 @@
 
 
 def expert_kernel(
-    line, cap_ref, ids_ref, score_ref, act_ref, wg_hbm, wu_hbm, wd_hbm, out_ref, mix_ref,
-    wg, wu, wd, gate_sum, up_sum, sent, xb, core_in, part,
+    line, cap_ref, ids_ref, score_ref, act_hbm, wg_hbm, wu_hbm, wd_hbm, out_ref, mix_ref,
+    act, wg, wu, wd, gate_sum, up_sum, sent, xb, core_in, part,
     side_in, up_in, down_in, stage, far_up, far_down, far_stage,
     w_sem, core_sem, up_sem, down_sem, side_sem, zrecv_sem, yrecv_sem,
     p_side_sem, p_side_recv, p_up_sem, p_up_recv, p_down_sem, p_down_recv, last_sem, last_recv,
-    far_sem,
+    far_sem, end_sem,
 ):
     node = lax.axis_index("node")
     ep = lax.axis_index("ep")
@@ -122,11 +122,13 @@
     to_side = {"ep": z * SIDE + other}
     to_up = {"ep": ep + SIDE}
     to_down = {"ep": ep - SIDE}
+    to_end = {"ep": (line - 1 - z) * SIDE + y}
     has_up, has_down = z < line - 1, z > 0
+    at_end = (z == 0) | (z == line - 1)
 
     loads = [
         pltpu.make_async_copy(src, dst, w_sem.at[i])
-        for i, (src, dst) in enumerate(((wg_hbm, wg), (wu_hbm, wu), (wd_hbm, wd)))
+        for i, (src, dst) in enumerate(((act_hbm, act), (wg_hbm, wg), (wu_hbm, wu), (wd_hbm, wd)))
     ]
     for load in loads:
         load.start()
@@ -142,6 +144,10 @@
     @pl.when(has_down)
     def _():
         pl.semaphore_signal(barrier, inc=1, device_id=to_down, device_id_type=MESH)
+
+    @pl.when(at_end)
+    def _():
+        pl.semaphore_signal(barrier, inc=1, device_id=to_end, device_id_type=MESH)
 
     def cols(c):
         return pl.ds(c * piece, piece)
@@ -181,16 +187,22 @@
     def x_far_down(o):
         return far(o, 1, to_down)
 
+    def x_end(c):
+        ref = xb.at[ep, :, cols(c)]
+        return remote(ref, ref, end_sem.at[c], zrecv_sem.at[z, c], to_end)
+
+    def x_far_end():
+        ref = xb.at[z * SIDE + other, :, cols(0)]
+        return remote(ref, ref, end_sem.at[pieces], far_sem.at[2, z], to_end)
+
     select, mix = select_rows(node, experts, ids_ref, score_ref, cap_ref)
     mix_ref[...] = mix
+    loads[0].wait()
     for c in range(pieces):
-        taken = lax.dot_general(
-            select, act_ref[:, cols(c)], (((0,), (0,)), ((), ())),
-            preferred_element_type=jnp.float32,
-        )
+        taken = jnp.dot(select, act[:, cols(c)], preferred_element_type=jnp.float32)
         sent[:, :, cols(c)] = taken.astype(sent.dtype).reshape(experts, rows, piece)
         if c == 0:
-            pl.semaphore_wait(barrier, 2 + has_up.astype(jnp.int32) + has_down.astype(jnp.int32))
+            pl.semaphore_wait(barrier, 4)
         core_copy(c).start()
     for c in range(pieces):
         core_copy(c).wait_recv()
@@ -203,35 +215,44 @@
     pl.when(has_up)(lambda: x_far_up(z).start())
     pl.when(has_down)(lambda: x_far_down(z).start())
 
+    @pl.when(at_end)
+    def _():
+        for c in range(pieces):
+            x_end(c).start()
+        x_far_end().start()
+
+    def relay(d, more):
+        return pl.when(more) if d < line - 2 else (lambda act: None)
+
     for d in range(1, line):
         for c in range(pieces):
             @pl.when(z - d >= 0)
             def _():
                 x_up(z - d, c).wait_recv()
-                pl.when(has_up)(lambda: x_up(z - d, c).start())
+                relay(d, has_up)(lambda: x_up(z - d, c).start())
                 if c > 0:
                     x_side(z - d, c).start()
 
             @pl.when(z + d < line)
             def _():
                 x_down(z + d, c).wait_recv()
-                pl.when(has_down)(lambda: x_down(z + d, c).start())
+                relay(d, has_down)(lambda: x_down(z + d, c).start())
                 if c > 0:
                     x_side(z + d, c).start()
 
         @pl.when(z - d >= 0)
         def _():
             x_far_up(z - d).wait_recv()
-            pl.when(has_up)(lambda: x_far_up(z - d).start())
+            relay(d, has_up)(lambda: x_far_up(z - d).start())
 
         @pl.when(z + d < line)
         def _():
             x_far_down(z + d).wait_recv()
-            pl.when(has_down)(lambda: x_far_down(z + d).start())
+            relay(d, has_down)(lambda: x_far_down(z + d).start())
 
     count = xb.shape[0] * rows
-    loads[0].wait()
     loads[1].wait()
+    loads[2].wait()
     for c in range(pieces):
         if c > 0:
             for o in range(line):
@@ -248,7 +269,7 @@
 
     gate = gate_sum[...]
     inner = (gate / (1.0 + jnp.exp(-gate)) * up_sum[...]).astype(jnp.bfloat16)
-    loads[2].wait()
+    loads[3].wait()
 
     def p_side(t, c):
         src = far_stage.at[t] if c == 0 else part.at[t * SIDE + other, :, cols(c)]
@@ -377,14 +398,14 @@
         by_place(lambda with_up, with_down: near_sum(c, with_up, with_down))
         last(c).start()
 
-    def done_far(t, upward):
-        pl.when(has_down if upward else has_up)(
+    def done_far(d, t, upward):
+        relay(d, has_down if upward else has_up)(
             lambda: (x_far_down if upward else x_far_up)(t).wait_send()
         )
         (p_far_up if upward else p_far_down)(t).wait_send()
 
-    def done(t, c, upward):
-        pl.when(has_down if upward else has_up)(
+    def done(d, t, c, upward):
+        relay(d, has_down if upward else has_up)(
             lambda: (x_down if upward else x_up)(t, c).wait_send()
         )
         if c > 0:
@@ -392,10 +413,16 @@
             p_side(t, c).wait_send()
         (p_up if upward else p_down)(t, c).wait_send()
 
+    @pl.when(at_end)
+    def _():
+        for c in range(pieces):
+            x_end(c).wait_send()
+        x_far_end().wait_send()
+
     pl.when(has_up)(lambda: x_far_up(z).wait_send())
     pl.when(has_down)(lambda: x_far_down(z).wait_send())
     for d in range(1, line):
-        at_distance(d, done_far)
+        at_distance(d, lambda t, upward: done_far(d, t, upward))
     for c in range(pieces):
         core_copy(c).wait_send()
         x_side(z, c).wait_send()
@@ -403,7 +430,7 @@
         pl.when(has_down)(lambda: x_down(z, c).wait_send())
         p_side(z, c).wait_send()
         for d in range(1, line):
-            at_distance(d, lambda t, upward: done(t, c, upward))
+            at_distance(d, lambda t, upward: done(d, t, c, upward))
     for c in order:
         last(c).wait_recv()
         last(c).wait_send()
@@ -427,13 +454,14 @@
         functools.partial(expert_kernel, line),
         out_shape=(
             jax.ShapeDtypeStruct((experts, rows, width), kind),
-            jax.ShapeDtypeStruct((tokens, experts * rows), jnp.bfloat16),
+            jax.ShapeDtypeStruct((experts * rows, tokens), jnp.bfloat16),
         ),
         in_specs=[pl.BlockSpec(memory_space=pltpu.SMEM)]
-        + [here] * 3
-        + [pl.BlockSpec(memory_space=pl.ANY)] * 3,
+        + [here] * 2
+        + [pl.BlockSpec(memory_space=pl.ANY)] * 4,
         out_specs=(here, here),
         scratch_shapes=[
+            vmem(activations.shape, kind),
             vmem(w_gate.shape, kind),
             vmem(w_up.shape, kind),
             vmem(w_down.shape, kind),
@@ -446,12 +474,12 @@
         ]
         + [vmem((line, rows, width), kind)] * 4
         + [vmem((line, rows, piece), kind)] * 3
-        + [sems((3,)), sems((2, pieces))]
+        + [sems((4,)), sems((2, pieces))]
         + [sems((line, pieces))] * 11
         + [sems((pieces,))] * 2
-        + [sems((7, line))],
+        + [sems((7, line)), sems((pieces + 1,))],
         compiler_params=pltpu.CompilerParams(
-            collective_id=0, has_side_effects=True, vmem_limit_bytes=48 * 1024 * 1024
+            collective_id=0, has_side_effects=True, vmem_limit_bytes=63 * 1024 * 1024
         ),
         cost_estimate=pl.CostEstimate(
             flops=6 * count * width * hidden,
@@ -459,16 +487,17 @@
             transcendentals=count * hidden,
         ),
         name="routed_experts",
-    )(capacity, expert_ids, route_scores, activations, w_gate, w_up, w_down)
+    )(capacity, expert_ids.T, route_scores.T, activations, w_gate, w_up, w_down)
 
 
 def grid_shards(activations, expert_ids, route_scores, capacity, w_gate, w_up, w_down):
     expert_out, combine_w = run_experts(
         activations, expert_ids, route_scores, capacity, w_gate, w_up, w_down
     )
-    mixed_out = jnp.dot(
+    mixed_out = lax.dot_general(
         combine_w,
         expert_out.reshape(-1, expert_out.shape[2]),
+        (((0,), (0,)), ((), ())),
         preferred_element_type=jnp.float32,
     )
     return mixed_out.astype(jnp.bfloat16)

time: 61 us -> 61.5 us (level)
  local copies, waits for them, and re-layouts: 5.61 us -> 0 us
  Pallas kernels: 53.5 us -> 58.6 us
  matrix products: 1.57 us -> 2.65 us
    unnamed x8 -> x0, local copies, waits for them, and re-layouts: 5.61 us -> none
    pallas_call x1, Pallas kernels: 53.5 us -> 58.6 us  [run_experts(): pl.pallas_call(functools.partial(expert_kernel, line), out_shape=(jax.Sha...]
    dot_general x1, matrix products: 1.57 us -> 2.65 us  [grid_shards(): lax.dot_general(combine_w, expert_out.reshape(-1, expert_out.shape[2]), (...]
where the time goes in v3:
time: 61.5 us; the launch traced here: 61.2 us
  Pallas kernels  58.6 us (95%)
  matrix products  2.65 us (4%)
    pallas_call x1, Pallas kernels, run_experts(): pl.pallas_call(functools.partial(expert_kernel, line), out_shape=(jax.Sha...  58.6 us
    dot_general x1, matrix products, grid_shards(): lax.dot_general(combine_w, expert_out.reshape(-1, expert_out.shape[2]), (...  2.65 us

profile of v3, /device:TPU:0, one launch (start us, length us, event | category | flops | bytes accessed | tf_op | source)
XLA Modules:
  0.0 61.2 jit_solution(13911361169034954248)
XLA Ops:
  0.0 58.6 %routed_experts.1 = (bf16[2,16,7168]{2,1,0:T(8,128)(2,1)}, bf16[32,96]{1,0:T(8,128)(2,1)}) custom-call(s32[256]{0:T(256)} %cap_ref.1, s32[8,96]{1,0:T(8,128)} %bitcast.6, f32[8,96]{1,0:T(8,128)} %bitcast.7, bf16[96,7168]{1,0:T(8,128)(2,1)} %act_hbm.1, bf16[7168,256]{1,0:T(8,128)(2,1)} %wg_hbm.1, bf16[7168,256]{1,0:T(8,128)(2,1)} %wu_hbm.1, ...), custom_call_target="tpu_custom_call" | custom-call | flops 1409286144 | bytes 11010048 | tf_op jit(solution)/shard_map/routed_experts/pallas_call | solution.py:453
  58.6 2.7 %convolution_convert_fusion = bf16[96,7168]{1,0:T(8,128)(2,1)} fusion(bf16[32,96]{1,0:T(8,128)(2,1)} %get-tuple-element.7, bf16[32,7168]{1,0:T(8,128)(2,1)} %bitcast.5), kind=kOutput, calls=%fused_computation | convolution fusion | flops 44728320 | bytes 1841152 | tf_op jit(solution)/shard_map/dot_general | solution.py:497

commit v4 on v3

--- a/solution.py
+++ b/solution.py
@@ -109,7 +109,7 @@
     side_in, up_in, down_in, stage, far_up, far_down, far_stage,
     w_sem, core_sem, up_sem, down_sem, side_sem, zrecv_sem, yrecv_sem,
     p_side_sem, p_side_recv, p_up_sem, p_up_recv, p_down_sem, p_down_recv, last_sem, last_recv,
-    far_sem, end_sem,
+    far_sem,
 ):
     node = lax.axis_index("node")
     ep = lax.axis_index("ep")
@@ -122,16 +122,13 @@
     to_side = {"ep": z * SIDE + other}
     to_up = {"ep": ep + SIDE}
     to_down = {"ep": ep - SIDE}
-    to_end = {"ep": (line - 1 - z) * SIDE + y}
     has_up, has_down = z < line - 1, z > 0
-    at_end = (z == 0) | (z == line - 1)
 
     loads = [
         pltpu.make_async_copy(src, dst, w_sem.at[i])
         for i, (src, dst) in enumerate(((act_hbm, act), (wg_hbm, wg), (wu_hbm, wu), (wd_hbm, wd)))
     ]
-    for load in loads:
-        load.start()
+    loads[0].start()
 
     barrier = pltpu.get_barrier_semaphore()
     pl.semaphore_signal(barrier, inc=1, device_id=to_core, device_id_type=MESH)
@@ -144,10 +141,6 @@
     @pl.when(has_down)
     def _():
         pl.semaphore_signal(barrier, inc=1, device_id=to_down, device_id_type=MESH)
-
-    @pl.when(at_end)
-    def _():
-        pl.semaphore_signal(barrier, inc=1, device_id=to_end, device_id_type=MESH)
 
     def cols(c):
         return pl.ds(c * piece, piece)
@@ -187,22 +180,16 @@
     def x_far_down(o):
         return far(o, 1, to_down)
 
-    def x_end(c):
-        ref = xb.at[ep, :, cols(c)]
-        return remote(ref, ref, end_sem.at[c], zrecv_sem.at[z, c], to_end)
-
-    def x_far_end():
-        ref = xb.at[z * SIDE + other, :, cols(0)]
-        return remote(ref, ref, end_sem.at[pieces], far_sem.at[2, z], to_end)
-
     select, mix = select_rows(node, experts, ids_ref, score_ref, cap_ref)
     mix_ref[...] = mix
     loads[0].wait()
+    for load in loads[1:]:
+        load.start()
     for c in range(pieces):
         taken = jnp.dot(select, act[:, cols(c)], preferred_element_type=jnp.float32)
         sent[:, :, cols(c)] = taken.astype(sent.dtype).reshape(experts, rows, piece)
         if c == 0:
-            pl.semaphore_wait(barrier, 4)
+            pl.semaphore_wait(barrier, 2 + has_up.astype(jnp.int32) + has_down.astype(jnp.int32))
         core_copy(c).start()
     for c in range(pieces):
         core_copy(c).wait_recv()
@@ -215,40 +202,31 @@
     pl.when(has_up)(lambda: x_far_up(z).start())
     pl.when(has_down)(lambda: x_far_down(z).start())
 
-    @pl.when(at_end)
-    def _():
-        for c in range(pieces):
-            x_end(c).start()
-        x_far_end().start()
-
-    def relay(d, more):
-        return pl.when(more) if d < line - 2 else (lambda act: None)
-
     for d in range(1, line):
         for c in range(pieces):
             @pl.when(z - d >= 0)
             def _():
                 x_up(z - d, c).wait_recv()
-                relay(d, has_up)(lambda: x_up(z - d, c).start())
+                pl.when(has_up)(lambda: x_up(z - d, c).start())
                 if c > 0:
                     x_side(z - d, c).start()
 
             @pl.when(z + d < line)
             def _():
                 x_down(z + d, c).wait_recv()
-                relay(d, has_down)(lambda: x_down(z + d, c).start())
+                pl.when(has_down)(lambda: x_down(z + d, c).start())
                 if c > 0:
                     x_side(z + d, c).start()
 
         @pl.when(z - d >= 0)
         def _():
             x_far_up(z - d).wait_recv()
-            relay(d, has_up)(lambda: x_far_up(z - d).start())
+            pl.when(has_up)(lambda: x_far_up(z - d).start())
 
         @pl.when(z + d < line)
         def _():
             x_far_down(z + d).wait_recv()
-            relay(d, has_down)(lambda: x_far_down(z + d).start())
+            pl.when(has_down)(lambda: x_far_down(z + d).start())
 
     count = xb.shape[0] * rows
     loads[1].wait()
@@ -398,14 +376,14 @@
         by_place(lambda with_up, with_down: near_sum(c, with_up, with_down))
         last(c).start()
 
-    def done_far(d, t, upward):
-        relay(d, has_down if upward else has_up)(
+    def done_far(t, upward):
+        pl.when(has_down if upward else has_up)(
             lambda: (x_far_down if upward else x_far_up)(t).wait_send()
         )
         (p_far_up if upward else p_far_down)(t).wait_send()
 
-    def done(d, t, c, upward):
-        relay(d, has_down if upward else has_up)(
+    def done(t, c, upward):
+        pl.when(has_down if upward else has_up)(
             lambda: (x_down if upward else x_up)(t, c).wait_send()
         )
         if c > 0:
@@ -413,16 +391,10 @@
             p_side(t, c).wait_send()
         (p_up if upward else p_down)(t, c).wait_send()
 
-    @pl.when(at_end)
-    def _():
-        for c in range(pieces):
-            x_end(c).wait_send()
-        x_far_end().wait_send()
-
     pl.when(has_up)(lambda: x_far_up(z).wait_send())
     pl.when(has_down)(lambda: x_far_down(z).wait_send())
     for d in range(1, line):
-        at_distance(d, lambda t, upward: done_far(d, t, upward))
+        at_distance(d, done_far)
     for c in range(pieces):
         core_copy(c).wait_send()
         x_side(z, c).wait_send()
@@ -430,7 +402,7 @@
         pl.when(has_down)(lambda: x_down(z, c).wait_send())
         p_side(z, c).wait_send()
         for d in range(1, line):
-            at_distance(d, lambda t, upward: done(d, t, c, upward))
+            at_distance(d, lambda t, upward: done(t, c, upward))
     for c in order:
         last(c).wait_recv()
         last(c).wait_send()
@@ -477,9 +449,9 @@
         + [sems((4,)), sems((2, pieces))]
         + [sems((line, pieces))] * 11
         + [sems((pieces,))] * 2
-        + [sems((7, line)), sems((pieces + 1,))],
+        + [sems((7, line))],
         compiler_params=pltpu.CompilerParams(
-            collective_id=0, has_side_effects=True, vmem_limit_bytes=63 * 1024 * 1024
+            collective_id=0, has_side_effects=True, vmem_limit_bytes=62 * 1024 * 1024 + 400 * 1024
         ),
         cost_estimate=pl.CostEstimate(
             flops=6 * count * width * hidden,

time: 61.5 us -> 57.1 us (0.928)
  Pallas kernels: 58.6 us -> 54.2 us
    pallas_call x1, Pallas kernels: 58.6 us -> 54.2 us  [run_experts(): pl.pallas_call(functools.partial(expert_kernel, line), out_shape=(jax.Sha...]
where the time goes in v4:
time: 57.1 us; the launch traced here: 56.9 us
  Pallas kernels  54.2 us (95%)
  matrix products  2.65 us (5%)
    pallas_call x1, Pallas kernels, run_experts(): pl.pallas_call(functools.partial(expert_kernel, line), out_shape=(jax.Sha...  54.2 us
    dot_general x1, matrix products, grid_shards(): lax.dot_general(combine_w, expert_out.reshape(-1, expert_out.shape[2]), (...  2.65 us

profile of v4, /device:TPU:0, one launch (start us, length us, event | category | flops | bytes accessed | tf_op | source)
XLA Modules:
  0.0 56.9 jit_solution(12154446900390793932)
XLA Ops:
  0.0 54.2 %routed_experts.1 = (bf16[2,16,7168]{2,1,0:T(8,128)(2,1)}, bf16[32,96]{1,0:T(8,128)(2,1)}) custom-call(s32[256]{0:T(256)} %cap_ref.1, s32[8,96]{1,0:T(8,128)} %bitcast.6, f32[8,96]{1,0:T(8,128)} %bitcast.7, bf16[96,7168]{1,0:T(8,128)(2,1)} %act_hbm.1, bf16[7168,256]{1,0:T(8,128)(2,1)} %wg_hbm.1, bf16[7168,256]{1,0:T(8,128)(2,1)} %wu_hbm.1, ...), custom_call_target="tpu_custom_call" | custom-call | flops 1409286144 | bytes 11010048 | tf_op jit(solution)/shard_map/routed_experts/pallas_call | solution.py:425
  54.2 2.7 %convolution_convert_fusion = bf16[96,7168]{1,0:T(8,128)(2,1)} fusion(bf16[32,96]{1,0:T(8,128)(2,1)} %get-tuple-element.7, bf16[32,7168]{1,0:T(8,128)(2,1)} %bitcast.5), kind=kOutput, calls=%fused_computation | convolution fusion | flops 44728320 | bytes 1841152 | tf_op jit(solution)/shard_map/dot_general | solution.py:469

commit v5 on v4

--- a/solution.py
+++ b/solution.py
@@ -109,7 +109,7 @@
     side_in, up_in, down_in, stage, far_up, far_down, far_stage,
     w_sem, core_sem, up_sem, down_sem, side_sem, zrecv_sem, yrecv_sem,
     p_side_sem, p_side_recv, p_up_sem, p_up_recv, p_down_sem, p_down_recv, last_sem, last_recv,
-    far_sem,
+    far_sem, near_sem, near_in, near_stage,
 ):
     node = lax.axis_index("node")
     ep = lax.axis_index("ep")
@@ -123,6 +123,12 @@
     to_up = {"ep": ep + SIDE}
     to_down = {"ep": ep - SIDE}
     has_up, has_down = z < line - 1, z > 0
+    at_end = (z == 0) | (z == line - 1)
+    blocks = xb.shape[0] // 2
+    half = z // (line // 2)
+    near = z + 1 - 2 * (z % 2)
+    to_near = {"ep": near * SIDE + y}
+    far_end, far_mid = (1 - half) * (line - 1), line // 2 - half
 
     loads = [
         pltpu.make_async_copy(src, dst, w_sem.at[i])
@@ -202,40 +208,92 @@
     pl.when(has_up)(lambda: x_far_up(z).start())
     pl.when(has_down)(lambda: x_far_down(z).start())
 
-    for d in range(1, line):
-        for c in range(pieces):
-            @pl.when(z - d >= 0)
-            def _():
-                x_up(z - d, c).wait_recv()
-                pl.when(has_up)(lambda: x_up(z - d, c).start())
-                if c > 0:
-                    x_side(z - d, c).start()
-
-            @pl.when(z + d < line)
-            def _():
-                x_down(z + d, c).wait_recv()
-                pl.when(has_down)(lambda: x_down(z + d, c).start())
-                if c > 0:
-                    x_side(z + d, c).start()
-
-        @pl.when(z - d >= 0)
-        def _():
-            x_far_up(z - d).wait_recv()
-            pl.when(has_up)(lambda: x_far_up(z - d).start())
-
-        @pl.when(z + d < line)
-        def _():
-            x_far_down(z + d).wait_recv()
-            pl.when(has_down)(lambda: x_far_down(z + d).start())
-
-    count = xb.shape[0] * rows
-    loads[1].wait()
-    loads[2].wait()
-    for c in range(pieces):
-        if c > 0:
-            for o in range(line):
-                x_side(o, c).wait_recv()
-        x = xb[:, :, cols(c)].reshape(count, piece)
+    def p_side(t, c, own=False):
+        src = part.at[t * SIDE + other, :, cols(c)]
+        if own:
+            src = far_stage.at[t] if c == 0 else near_stage.at[:, cols(c)]
+        return remote(
+            src, side_in.at[t, :, cols(c)],
+            p_side_sem.at[t, c], p_side_recv.at[t, c], to_side,
+        )
+
+    def p_up(t, c):
+        return remote(
+            stage.at[t, :, cols(c)], up_in.at[t, :, cols(c)],
+            p_up_sem.at[t, c], p_up_recv.at[t, c], to_up,
+        )
+
+    def p_down(t, c):
+        return remote(
+            stage.at[t, :, cols(c)], down_in.at[t, :, cols(c)],
+            p_down_sem.at[t, c], p_down_recv.at[t, c], to_down,
+        )
+
+    def p_far_up(t):
+        return remote(far_stage.at[t], far_up.at[t], far_sem.at[3, t], far_sem.at[4, t], to_up)
+
+    def p_far_down(t):
+        return remote(far_stage.at[t], far_down.at[t], far_sem.at[5, t], far_sem.at[6, t], to_down)
+
+    def p_near(c):
+        return remote(
+            part.at[near * SIDE + other, :, cols(c)], near_in.at[:, cols(c)],
+            near_sem.at[0, c], near_sem.at[1, c], to_near,
+        )
+
+    def last(c):
+        ref = out_ref.at[node, :, cols(c)]
+        return remote(ref, ref, last_sem.at[c], last_recv.at[c], to_core)
+
+    def at_distance(d, act):
+        pl.when(z + d < line)(lambda: act(z + d, True))
+        pl.when(z - d >= 0)(lambda: act(z - d, False))
+
+    def f32(ref, t, c):
+        return ref[t, :, cols(c)].astype(jnp.float32)
+
+    def there(t):
+        return f32(part, t * SIDE + other, 0)
+
+    def pass_on(t, c, upward, across):
+        across = across and c > 0
+        if across:
+            p_side(t, c).wait_recv()
+        copy, arrived = (p_up, up_in) if upward else (p_down, down_in)
+        more, end = (has_down, z == 0) if upward else (has_up, z == line - 1)
+
+        def here():
+            own = f32(part, t * SIDE + y, c)
+            return own + f32(side_in, t, c) if across else own
+
+        @pl.when(more)
+        def _():
+            copy(t, c).wait_recv()
+            stage[t, :, cols(c)] = (here() + f32(arrived, t, c)).astype(stage.dtype)
+
+        @pl.when(end)
+        def _():
+            stage[t, :, cols(c)] = here().astype(stage.dtype)
+
+        copy(t, c).start()
+
+    def pass_far(t, upward):
+        copy, arrived = (p_far_up, far_up) if upward else (p_far_down, far_down)
+        more, end = (has_down, z == 0) if upward else (has_up, z == line - 1)
+
+        @pl.when(more)
+        def _():
+            copy(t).wait_recv()
+            far_stage[t] = (there(t) + arrived[t].astype(jnp.float32)).astype(far_stage.dtype)
+
+        @pl.when(end)
+        def _():
+            far_stage[t] = there(t).astype(far_stage.dtype)
+
+        copy(t).start()
+
+    def add_gate_up(start, c):
+        x = xb[pl.ds(start, blocks), :, cols(c)].reshape(blocks * rows, piece)
         gate_part = jnp.dot(x, wg[cols(c), :], preferred_element_type=jnp.float32)
         up_part = jnp.dot(x, wu[cols(c), :], preferred_element_type=jnp.float32)
         if c == 0:
@@ -245,104 +303,127 @@
             gate_sum[...] += gate_part
             up_sum[...] += up_part
 
-    gate = gate_sum[...]
-    inner = (gate / (1.0 + jnp.exp(-gate)) * up_sum[...]).astype(jnp.bfloat16)
-    loads[3].wait()
-
-    def p_side(t, c):
-        src = far_stage.at[t] if c == 0 else part.at[t * SIDE + other, :, cols(c)]
-        return remote(
-            src, side_in.at[t, :, cols(c)],
-            p_side_sem.at[t, c], p_side_recv.at[t, c], to_side,
-        )
-
-    def p_up(t, c):
-        return remote(
-            stage.at[t, :, cols(c)], up_in.at[t, :, cols(c)],
-            p_up_sem.at[t, c], p_up_recv.at[t, c], to_up,
-        )
-
-    def p_down(t, c):
-        return remote(
-            stage.at[t, :, cols(c)], down_in.at[t, :, cols(c)],
-            p_down_sem.at[t, c], p_down_recv.at[t, c], to_down,
-        )
-
-    def p_far_up(t):
-        return remote(far_stage.at[t], far_up.at[t], far_sem.at[3, t], far_sem.at[4, t], to_up)
-
-    def p_far_down(t):
-        return remote(far_stage.at[t], far_down.at[t], far_sem.at[5, t], far_sem.at[6, t], to_down)
-
-    def last(c):
-        ref = out_ref.at[node, :, cols(c)]
-        return remote(ref, ref, last_sem.at[c], last_recv.at[c], to_core)
-
-    def at_distance(d, act):
-        pl.when(z + d < line)(lambda: act(z + d, True))
-        pl.when(z - d >= 0)(lambda: act(z - d, False))
-
-    def f32(ref, t, c):
-        return ref[t, :, cols(c)].astype(jnp.float32)
-
-    def here(t, c):
-        own = f32(part, t * SIDE + y, c)
-        return own if c == 0 else own + f32(side_in, t, c)
-
-    def there(t):
-        return f32(part, t * SIDE + other, 0)
-
-    def pass_on(t, c, upward):
+    def swiglu():
+        gate = gate_sum[...]
+        return (gate / (1.0 + jnp.exp(-gate)) * up_sum[...]).astype(jnp.bfloat16)
+
+    def put_partial(inner, start, c):
+        value = jnp.dot(inner, wd[:, cols(c)], preferred_element_type=jnp.float32)
+        part[pl.ds(start, blocks), :, cols(c)] = value.astype(part.dtype).reshape(
+            blocks, rows, piece
+        )
+
+    def send_near(c):
         if c > 0:
-            p_side(t, c).wait_recv()
-        copy, arrived = (p_up, up_in) if upward else (p_down, down_in)
-        more, end = (has_down, z == 0) if upward else (has_up, z == line - 1)
-
-        @pl.when(more)
-        def _():
-            copy(t, c).wait_recv()
-            stage[t, :, cols(c)] = (here(t, c) + f32(arrived, t, c)).astype(stage.dtype)
-
-        @pl.when(end)
-        def _():
-            stage[t, :, cols(c)] = here(t, c).astype(stage.dtype)
-
-        copy(t, c).start()
-
-    def pass_far(t, upward):
-        copy, arrived = (p_far_up, far_up) if upward else (p_far_down, far_down)
-        more, end = (has_down, z == 0) if upward else (has_up, z == line - 1)
-
-        @pl.when(more)
-        def _():
-            copy(t).wait_recv()
-            far_stage[t] = (there(t) + arrived[t].astype(jnp.float32)).astype(far_stage.dtype)
-
-        @pl.when(end)
-        def _():
-            far_stage[t] = there(t).astype(far_stage.dtype)
-
-        copy(t).start()
+            p_near(c).start()
+
+        @pl.when(z == 0)
+        def _():
+            pass_on(z + 1, c, True, False)
+            if c == 0:
+                pass_far(z + 1, True)
+
+        @pl.when(z == line - 1)
+        def _():
+            pass_on(z - 1, c, False, False)
+            if c == 0:
+                pass_far(z - 1, False)
+
+    inner = None
+    for d in range(1, line):
+        if d == line - 1:
+            inner = swiglu()
+            loads[3].wait()
+        for c in range(pieces):
+            @pl.when(z - d >= 0)
+            def _():
+                x_up(z - d, c).wait_recv()
+                pl.when(has_up)(lambda: x_up(z - d, c).start())
+                if c > 0:
+                    x_side(z - d, c).start()
+
+            @pl.when(z + d < line)
+            def _():
+                x_down(z + d, c).wait_recv()
+                pl.when(has_down)(lambda: x_down(z + d, c).start())
+                if c > 0:
+                    x_side(z + d, c).start()
+
+            if d == line - 2:
+                if c == 0:
+                    loads[1].wait()
+                    loads[2].wait()
+                else:
+                    x_side(z, c).wait_recv()
+                    x_side(near, c).wait_recv()
+                add_gate_up(half * blocks, c)
+            if d == line - 1:
+                put_partial(inner, half * blocks, c)
+                pl.when(at_end)(lambda: send_near(c))
+
+        @pl.when(z - d >= 0)
+        def _():
+            x_far_up(z - d).wait_recv()
+            pl.when(has_up)(lambda: x_far_up(z - d).start())
+
+        @pl.when(z + d < line)
+        def _():
+            x_far_down(z + d).wait_recv()
+            pl.when(has_down)(lambda: x_far_down(z + d).start())
+
+    for c in range(pieces):
+        if c > 0:
+            x_side(far_end, c).wait_recv()
+            x_side(far_mid, c).wait_recv()
+        add_gate_up((1 - half) * blocks, c)
+    inner = swiglu()
 
     order = list(range(1, pieces)) + [0]
     for c in order:
-        value = jnp.dot(inner, wd[:, cols(c)], preferred_element_type=jnp.float32)
-        part[:, :, cols(c)] = value.astype(part.dtype).reshape(part.shape[0], rows, piece)
+        put_partial(inner, (1 - half) * blocks, c)
         if c > 0:
-            at_distance(line - 1, lambda t, upward: p_side(t, c).start())
-            if line > 2:
-                at_distance(line - 2, lambda t, upward: p_side(t, c).start())
-    for d in range(line - 3, 0, -1):
-        for c in range(1, pieces):
-            at_distance(d, lambda t, upward: p_side(t, c).start())
+            p_side(far_end, c).start()
+
+            @pl.when(jnp.logical_not(at_end))
+            def _():
+                p_near(c).start()
+
     for c in range(1, pieces):
-        p_side(z, c).start()
-
-    for d in range(line - 1, 0, -1):
-        at_distance(d, lambda t, upward: pass_on(t, 0, upward))
+        p_side(far_mid, c).start()
+
+    for d in range(line - 1, 1, -1):
+        at_distance(d, lambda t, upward: pass_on(t, 0, upward, True))
         at_distance(d, pass_far)
         for c in range(1, pieces):
-            at_distance(d, lambda t, upward: pass_on(t, c, upward))
+            at_distance(d, lambda t, upward: pass_on(t, c, upward, True))
+        if d == line - 1:
+            for c in range(1, pieces):
+                p_near(c).wait_recv()
+                total = f32(part, z * SIDE + other, c) + near_in[:, cols(c)].astype(jnp.float32)
+                near_stage[:, cols(c)] = total.astype(near_stage.dtype)
+                p_side(z, c, True).start()
+
+    @pl.when(z == line // 2 - 1)
+    def _():
+        pass_on(z - 1, 0, False, False)
+        pass_far(z - 1, False)
+        pass_on(z + 1, 0, True, True)
+        pass_far(z + 1, True)
+        for c in range(1, pieces):
+            pass_on(z - 1, c, False, False)
+        for c in range(1, pieces):
+            pass_on(z + 1, c, True, True)
+
+    @pl.when(z == line // 2)
+    def _():
+        pass_on(z + 1, 0, True, False)
+        pass_far(z + 1, True)
+        pass_on(z - 1, 0, False, True)
+        pass_far(z - 1, False)
+        for c in range(1, pieces):
+            pass_on(z + 1, c, True, False)
+        for c in range(1, pieces):
+            pass_on(z - 1, c, False, True)
 
     def far_sum(with_up, with_down):
         total = there(z)
@@ -352,7 +433,7 @@
             total = total + far_down[z].astype(jnp.float32)
         far_stage[z] = total.astype(far_stage.dtype)
 
-    def near_sum(c, with_up, with_down):
+    def finish(c, with_up, with_down):
         total = f32(part, ep, c) + f32(side_in, z, c)
         if with_up:
             total = total + f32(up_in, z, c)
@@ -368,12 +449,12 @@
     pl.when(has_down)(lambda: p_far_up(z).wait_recv())
     pl.when(has_up)(lambda: p_far_down(z).wait_recv())
     by_place(far_sum)
-    p_side(z, 0).start()
+    p_side(z, 0, True).start()
     for c in order:
-        p_side(z, c).wait_recv()
+        p_side(z, c, True).wait_recv()
         pl.when(has_down)(lambda: p_up(z, c).wait_recv())
         pl.when(has_up)(lambda: p_down(z, c).wait_recv())
-        by_place(lambda with_up, with_down: near_sum(c, with_up, with_down))
+        by_place(lambda with_up, with_down: finish(c, with_up, with_down))
         last(c).start()
 
     def done_far(t, upward):
@@ -388,7 +469,6 @@
         )
         if c > 0:
             x_side(t, c).wait_send()
-            p_side(t, c).wait_send()
         (p_up if upward else p_down)(t, c).wait_send()
 
     pl.when(has_up)(lambda: x_far_up(z).wait_send())
@@ -400,7 +480,11 @@
         x_side(z, c).wait_send()
         pl.when(has_up)(lambda: x_up(z, c).wait_send())
         pl.when(has_down)(lambda: x_down(z, c).wait_send())
-        p_side(z, c).wait_send()
+        p_side(z, c, True).wait_send()
+        if c > 0:
+            p_near(c).wait_send()
+            p_side(far_end, c).wait_send()
+            p_side(far_mid, c).wait_send()
         for d in range(1, line):
             at_distance(d, lambda t, upward: done(t, c, upward))
     for c in order:
@@ -437,8 +521,8 @@
             vmem(w_gate.shape, kind),
             vmem(w_up.shape, kind),
             vmem(w_down.shape, kind),
-            vmem((count, hidden), jnp.float32),
-            vmem((count, hidden), jnp.float32),
+            vmem((count // 2, hidden), jnp.float32),
+            vmem((count // 2, hidden), jnp.float32),
             vmem((experts, rows, width), kind),
             vmem((n_ep, rows, width), kind),
             vmem((rows, width), kind),
@@ -449,7 +533,7 @@
         + [sems((4,)), sems((2, pieces))]
         + [sems((line, pieces))] * 11
         + [sems((pieces,))] * 2
-        + [sems((7, line))],
+        + [sems((7, line)), sems((2, pieces)), vmem((rows, width), kind), vmem((rows, width), kind)],
         compiler_params=pltpu.CompilerParams(
             collective_id=0, has_side_effects=True, vmem_limit_bytes=62 * 1024 * 1024 + 400 * 1024
         ),

time: 57.1 us -> 52.9 us (0.926)
  Pallas kernels: 54.2 us -> 50 us
    pallas_call x1, Pallas kernels: 54.2 us -> 50 us  [run_experts(): pl.pallas_call(functools.partial(expert_kernel, line), out_shape=(jax.Sha...]
where the time goes in v5:
time: 52.9 us; the launch traced here: 52.6 us
  Pallas kernels  50 us (95%)
  matrix products  2.65 us (5%)
    pallas_call x1, Pallas kernels, run_experts(): pl.pallas_call(functools.partial(expert_kernel, line), out_shape=(jax.Sha...  50 us
    dot_general x1, matrix products, grid_shards(): lax.dot_general(combine_w, expert_out.reshape(-1, expert_out.shape[2]), (...  2.65 us

profile of v5, /device:TPU:0, one launch (start us, length us, event | category | flops | bytes accessed | tf_op | source)
XLA Modules:
  0.0 52.6 jit_solution(5020742535219979073)
XLA Ops:
  0.0 50.0 %routed_experts.1 = (bf16[2,16,7168]{2,1,0:T(8,128)(2,1)}, bf16[32,96]{1,0:T(8,128)(2,1)}) custom-call(s32[256]{0:T(256)} %cap_ref.1, s32[8,96]{1,0:T(8,128)} %bitcast.6, f32[8,96]{1,0:T(8,128)} %bitcast.7, bf16[96,7168]{1,0:T(8,128)(2,1)} %act_hbm.1, bf16[7168,256]{1,0:T(8,128)(2,1)} %wg_hbm.1, bf16[7168,256]{1,0:T(8,128)(2,1)} %wu_hbm.1, ...), custom_call_target="tpu_custom_call" | custom-call | flops 1409286144 | bytes 11010048 | tf_op jit(solution)/shard_map/routed_experts/pallas_call | solution.py:509
  50.0 2.6 %convolution_convert_fusion = bf16[96,7168]{1,0:T(8,128)(2,1)} fusion(bf16[32,96]{1,0:T(8,128)(2,1)} %get-tuple-element.7, bf16[32,7168]{1,0:T(8,128)(2,1)} %bitcast.5), kind=kOutput, calls=%fused_computation | convolution fusion | flops 44728320 | bytes 1841152 | tf_op jit(solution)/shard_map/dot_general | solution.py:553

commit v6 on v5

--- a/solution.py
+++ b/solution.py
@@ -65,10 +65,10 @@
 
 
 def piece_of(width):
-    for size in (1024, 512, 256):
-        if width % size == 0:
-            return size
-    return 128
+    for parts in (4, 2):
+        if width % (parts * 128) == 0:
+            return width // parts
+    return width
 
 
 def select_rows(node, experts, ids_ref, score_ref, cap_ref):

time: 52.9 us -> 55 us (1.040)
  Pallas kernels: 50 us -> 51.8 us
    pallas_call x1, Pallas kernels: 50 us -> 51.8 us  [run_experts(): pl.pallas_call(functools.partial(expert_kernel, line), out_shape=(jax.Sha...]
where the time goes in v6:
time: 55 us; the launch traced here: 54.4 us
  Pallas kernels  51.8 us (94%)
  matrix products  2.66 us (5%)
    pallas_call x1, Pallas kernels, run_experts(): pl.pallas_call(functools.partial(expert_kernel, line), out_shape=(jax.Sha...  51.8 us
    dot_general x1, matrix products, grid_shards(): lax.dot_general(combine_w, expert_out.reshape(-1, expert_out.shape[2]), (...  2.66 us

profile of v6, /device:TPU:0, one launch (start us, length us, event | category | flops | bytes accessed | tf_op | source)
XLA Modules:
  0.0 54.4 jit_solution(748720964069003156)
XLA Ops:
  0.0 51.8 %routed_experts.1 = (bf16[2,16,7168]{2,1,0:T(8,128)(2,1)}, bf16[32,96]{1,0:T(8,128)(2,1)}) custom-call(s32[256]{0:T(256)} %cap_ref.1, s32[8,96]{1,0:T(8,128)} %bitcast.6, f32[8,96]{1,0:T(8,128)} %bitcast.7, bf16[96,7168]{1,0:T(8,128)(2,1)} %act_hbm.1, bf16[7168,256]{1,0:T(8,128)(2,1)} %wg_hbm.1, bf16[7168,256]{1,0:T(8,128)(2,1)} %wu_hbm.1, ...), custom_call_target="tpu_custom_call" | custom-call | flops 1409286144 | bytes 11010048 | tf_op jit(solution)/shard_map/routed_experts/pallas_call | solution.py:509
  51.8 2.7 %convolution_convert_fusion = bf16[96,7168]{1,0:T(8,128)(2,1)} fusion(bf16[32,96]{1,0:T(8,128)(2,1)} %get-tuple-element.7, bf16[32,7168]{1,0:T(8,128)(2,1)} %bitcast.5), kind=kOutput, calls=%fused_computation | convolution fusion | flops 44728320 | bytes 1841152 | tf_op jit(solution)/shard_map/dot_general | solution.py:553

commit v7 on v5

--- a/solution.py
+++ b/solution.py
@@ -104,12 +104,12 @@
 
 
 def expert_kernel(
-    line, cap_ref, ids_ref, score_ref, act_hbm, wg_hbm, wu_hbm, wd_hbm, out_ref, mix_ref,
+    line, cap_ref, ids_ref, score_ref, act_hbm, wg_hbm, wu_hbm, wd_hbm, out_hbm,
     act, wg, wu, wd, gate_sum, up_sum, sent, xb, core_in, part,
     side_in, up_in, down_in, stage, far_up, far_down, far_stage,
     w_sem, core_sem, up_sem, down_sem, side_sem, zrecv_sem, yrecv_sem,
     p_side_sem, p_side_recv, p_up_sem, p_up_recv, p_down_sem, p_down_recv, last_sem, last_recv,
-    far_sem, near_sem, near_in, near_stage,
+    far_sem, near_sem, near_in, near_stage, out_ref, mixed, out_sem,
 ):
     node = lax.axis_index("node")
     ep = lax.axis_index("ep")
@@ -187,7 +187,6 @@
         return far(o, 1, to_down)
 
     select, mix = select_rows(node, experts, ids_ref, score_ref, cap_ref)
-    mix_ref[...] = mix
     loads[0].wait()
     for load in loads[1:]:
         load.start()
@@ -456,6 +455,20 @@
         pl.when(has_up)(lambda: p_down(z, c).wait_recv())
         by_place(lambda with_up, with_down: finish(c, with_up, with_down))
         last(c).start()
+
+    def put_out(c):
+        return pltpu.make_async_copy(
+            mixed.at[:, cols(c)], out_hbm.at[:, cols(c)], out_sem.at[c]
+        )
+
+    for c in order:
+        last(c).wait_recv()
+        value = lax.dot_general(
+            mix, out_ref[:, :, cols(c)].reshape(experts * rows, piece), (((0,), (0,)), ((), ())),
+            preferred_element_type=jnp.float32,
+        )
+        mixed[:, cols(c)] = value.astype(mixed.dtype)
+        put_out(c).start()
 
     def done_far(t, upward):
         pl.when(has_down if upward else has_up)(
@@ -488,8 +501,8 @@
         for d in range(1, line):
             at_distance(d, lambda t, upward: done(t, c, upward))
     for c in order:
-        last(c).wait_recv()
         last(c).wait_send()
+        put_out(c).wait()
 
 
 def run_experts(activations, expert_ids, route_scores, capacity, w_gate, w_up, w_down):
@@ -508,14 +521,11 @@
     here = pl.BlockSpec(memory_space=pltpu.VMEM)
     return pl.pallas_call(
         functools.partial(expert_kernel, line),
-        out_shape=(
-            jax.ShapeDtypeStruct((experts, rows, width), kind),
-            jax.ShapeDtypeStruct((experts * rows, tokens), jnp.bfloat16),
-        ),
+        out_shape=jax.ShapeDtypeStruct((tokens, width), kind),
         in_specs=[pl.BlockSpec(memory_space=pltpu.SMEM)]
         + [here] * 2
         + [pl.BlockSpec(memory_space=pl.ANY)] * 4,
-        out_specs=(here, here),
+        out_specs=pl.BlockSpec(memory_space=pl.ANY),
         scratch_shapes=[
             vmem(activations.shape, kind),
             vmem(w_gate.shape, kind),
@@ -533,7 +543,8 @@
         + [sems((4,)), sems((2, pieces))]
         + [sems((line, pieces))] * 11
         + [sems((pieces,))] * 2
-        + [sems((7, line)), sems((2, pieces)), vmem((rows, width), kind), vmem((rows, width), kind)],
+        + [sems((7, line)), sems((2, pieces)), vmem((rows, width), kind), vmem((rows, width), kind)]
+        + [vmem((experts, rows, width), kind), vmem((tokens, width), kind), sems((pieces,))],
         compiler_params=pltpu.CompilerParams(
             collective_id=0, has_side_effects=True, vmem_limit_bytes=62 * 1024 * 1024 + 400 * 1024
         ),
@@ -547,16 +558,9 @@
 
 
 def grid_shards(activations, expert_ids, route_scores, capacity, w_gate, w_up, w_down):
-    expert_out, combine_w = run_experts(
+    return run_experts(
         activations, expert_ids, route_scores, capacity, w_gate, w_up, w_down
     )
-    mixed_out = lax.dot_general(
-        combine_w,
-        expert_out.reshape(-1, expert_out.shape[2]),
-        (((0,), (0,)), ((), ())),
-        preferred_element_type=jnp.float32,
-    )
-    return mixed_out.astype(jnp.bfloat16)
 
 
 def solution(mesh):

time: 52.9 us -> 53.2 us (level)
  matrix products: 2.65 us -> 0 us
  local copies, waits for them, and re-layouts: 0 us -> 2.51 us
    dot_general x1 -> x0, matrix products: 2.65 us -> none  [grid_shards(): lax.dot_general(combine_w, expert_out.reshape(-1, expert_out.shape[2]), (...]
    unnamed x0 -> x1, local copies, waits for them, and re-layouts: none -> 2.51 us
where the time goes in v7:
time: 53.2 us; the launch traced here: 53 us
  Pallas kernels  50.5 us (95%)
  local copies, waits for them, and re-layouts  2.51 us (5%)
    pallas_call x1, Pallas kernels, run_experts(): pl.pallas_call(functools.partial(expert_kernel, line), out_shape=jax.Shap...  50.5 us
    unnamed x1, local copies, waits for them, and re-layouts  2.51 us

profile of v7, /device:TPU:0, one launch (start us, length us, event | category | flops | bytes accessed | tf_op | source)
XLA Modules:
  0.0 53.0 jit_solution(9309719391420796238)
XLA Ops:
  0.0 50.5 %routed_experts.1 = bf16[96,7168]{1,0:T(8,128)(2,1)} custom-call(s32[256]{0:T(256)} %cap_ref.1, s32[8,96]{1,0:T(8,128)} %bitcast.2, f32[8,96]{1,0:T(8,128)} %bitcast.3, bf16[96,7168]{1,0:T(8,128)(2,1)} %act_hbm.1, bf16[7168,256]{1,0:T(8,128)(2,1)} %wg_hbm.1, bf16[7168,256]{1,0:T(8,128)(2,1)} %wu_hbm.1, bf16[256,7168]{1,0:T(8,128)(2,1)} %wd_hbm.1), custom_call_target="tpu_custom_call" | custom-call | flops 1409286144 | bytes 11010048 | tf_op jit(solution)/shard_map/routed_experts/pallas_call | solution.py:522
  50.5 2.5 %copy.9 = bf16[96,7168]{1,0:T(8,128)(2,1)} copy(bf16[96,7168]{1,0:T(8,128)(2,1)} %routed_experts.1) | data formatting | bytes 2752512

commit v8 on v5

--- a/solution.py
+++ b/solution.py
@@ -200,9 +200,9 @@
     for c in range(pieces):
         core_copy(c).wait_recv()
         xb[ep, :, cols(c)] = sent[node, :, cols(c)] + core_in[:, cols(c)]
-        x_side(z, c).start()
         pl.when(has_up)(lambda: x_up(z, c).start())
         pl.when(has_down)(lambda: x_down(z, c).start())
+        x_side(z, c).start()
 
     x_side(z, 0).wait_recv()
     pl.when(has_up)(lambda: x_far_up(z).start())
@@ -535,7 +535,7 @@
         + [sems((pieces,))] * 2
         + [sems((7, line)), sems((2, pieces)), vmem((rows, width), kind), vmem((rows, width), kind)],
         compiler_params=pltpu.CompilerParams(
-            collective_id=0, has_side_effects=True, vmem_limit_bytes=62 * 1024 * 1024 + 400 * 1024
+            collective_id=0, has_side_effects=True, vmem_limit_bytes=61 * 1024 * 1024 + 768 * 1024
         ),
         cost_estimate=pl.CostEstimate(
             flops=6 * count * width * hidden,

time: 52.9 us -> 52.9 us (level)
  no operation moved by 1% of the time
where the time goes in v8:
time: 52.9 us; the launch traced here: 52.6 us
  Pallas kernels  50 us (95%)
  matrix products  2.65 us (5%)
    pallas_call x1, Pallas kernels, run_experts(): pl.pallas_call(functools.partial(expert_kernel, line), out_shape=(jax.Sha...  50 us
    dot_general x1, matrix products, grid_shards(): lax.dot_general(combine_w, expert_out.reshape(-1, expert_out.shape[2]), (...  2.65 us

profile of v8, /device:TPU:0, one launch (start us, length us, event | category | flops | bytes accessed | tf_op | source)
XLA Modules:
  0.0 52.6 jit_solution(10863657051735938682)
XLA Ops:
  0.0 50.0 %routed_experts.1 = (bf16[2,16,7168]{2,1,0:T(8,128)(2,1)}, bf16[32,96]{1,0:T(8,128)(2,1)}) custom-call(s32[256]{0:T(256)} %cap_ref.1, s32[8,96]{1,0:T(8,128)} %bitcast.6, f32[8,96]{1,0:T(8,128)} %bitcast.7, bf16[96,7168]{1,0:T(8,128)(2,1)} %act_hbm.1, bf16[7168,256]{1,0:T(8,128)(2,1)} %wg_hbm.1, bf16[7168,256]{1,0:T(8,128)(2,1)} %wu_hbm.1, ...), custom_call_target="tpu_custom_call" | custom-call | flops 1409286144 | bytes 11010048 | tf_op jit(solution)/shard_map/routed_experts/pallas_call | solution.py:509
  50.0 2.6 %convolution_convert_fusion = bf16[96,7168]{1,0:T(8,128)(2,1)} fusion(bf16[32,96]{1,0:T(8,128)(2,1)} %get-tuple-element.7, bf16[32,7168]{1,0:T(8,128)(2,1)} %bitcast.5), kind=kOutput, calls=%fused_computation | convolution fusion | flops 44728320 | bytes 1841152 | tf_op jit(solution)/shard_map/dot_general | solution.py:553
